TPU v7x, 512 devices: a whole 4x4x16 slice. The times are simulated.
512 devices in a mesh: gx: 8 (over y, core), yz: 32 (over z_lo, x), ta: 2 (over z_hi).
Axes of the slice: x: 4, y: 4, z: 16 (z_hi: 2, z_lo: 8; z = z_hi * 8 + z_lo), core: 2. Of those that a mesh axis runs over, the one named last changes fastest.
Arguments:
- field: float32 [4, 4, 512, 32768], P('ta', None, 'gx', 'yz'), may hold values from -20 to 20
- start: float32 [512, 64], replicated, may hold values from -6 to 6
Outputs:
- core: float32 [4, 4, 64, 32768], P('ta', None, 'gx', 'yz')
All inputs are finite; a program needn't handle non-finite values.
Results may differ from a plain program's by a relative error of at most 0.0003.
Values sent between devices are 32-bit elements; how exact they have to be, the bound alone decides.
No kernel may reach another device: no remote copies, remote signals or barrier semaphores. Data moves between devices by JAX's collectives and lax.ppermute only.
A program may use at most 64 MiB of HBM per device.

v0:
```python
import jax
import jax.numpy as jnp
from jax import lax
from jax.sharding import PartitionSpec as P

ITERS = 2


def orthonormal(image):
    small = jnp.dot(image.T, image, precision=lax.Precision.HIGHEST)
    lower = jnp.linalg.cholesky(small)
    return lax.linalg.triangular_solve(lower, image, left_side=False, lower=True, transpose_a=True)


def shards(field, start):
    wide = lax.all_to_all(field, "gx", split_axis=3, concat_axis=2, tiled=True)
    partial_gram = lax.dot_general(
        wide, wide, (((0, 1, 3), (0, 1, 3)), ((), ())), precision=lax.Precision.HIGHEST
    )
    gram = lax.psum(partial_gram, ("gx", "yz", "ta"))
    count = (
        field.shape[0] * field.shape[1] * field.shape[3] * lax.axis_size("yz") * lax.axis_size("ta")
    )
    gram = gram / jnp.float32(count)
    basis = start
    for step in range(ITERS):
        basis = orthonormal(jnp.dot(gram, basis, precision=lax.Precision.HIGHEST))
    plane_core = jnp.einsum("ir,tsip->tsrp", basis, wide, precision=lax.Precision.HIGHEST)
    core = lax.all_to_all(plane_core, "gx", split_axis=2, concat_axis=3, tiled=True)
    return core


def solution(mesh):
    placed = (P("ta", None, "gx", "yz"), P())
    return jax.shard_map(
        shards, mesh=mesh, in_specs=placed, out_specs=P("ta", None, "gx", "yz"), check_vma=False
    )
```

profile of v0, /device:TPU:1, one launch (start us, length us, event | category | flops | bytes accessed | tf_op | source)
XLA Modules:
  0.0 590.0 jit_solution(6245925026930584702)
XLA Ops:
  6.5 0.0 copy-start
  6.5 0.0 all-reduce.2.cloned.1.call-start
  6.5 4.8 copy.6
  11.4 6.8 %reshape.19 = f32[8,1,65536]{2,1,0:T(1,128)S(1)} reshape(f32[1024,2,4,64]{3,2,1,0:T(4,128)} %bitcast.59) | data formatting | bytes 4194304
  18.2 36.5 %all_to_all.36 = f32[8,1,65536]{2,1,0:T(1,128)} all-to-all(f32[8,1,65536]{2,1,0:T(1,128)S(1)} %reshape.19), channel_id=1, replica_groups=mesh['gx'=8,'yz'=32,'ta'=2] {'gx'}, dimensions={0} | all-to-all | bytes 4194304 | tf_op jit(solution)/shard_map/all_to_all | solution.py:16
  54.7 0.5 broadcast.36
  55.2 7.2 %reduce.4 = f32[8,65536]{1,0:T(8,128)S(1)} reduce(f32[8,1,65536]{2,1,0:T(1,128)} %all_to_all.36, f32[]{:T(128)} %broadcast.36), dimensions={1}, to_apply=%all_to_all.26.reduce_sub_computation | reduce | bytes 4194308 | tf_op jit(solution)/shard_map/all_to_all | solution.py:16
  62.4 4.8 reshape.20
  67.2 3.7 copy.7
  70.9 4.6 convolution_bitcast_fusion
  75.5 0.0 all-reduce.2.cloned.1.call-update
  75.5 465.5 %all-reduce.2.cloned.1.call-done = f32[512,512]{1,0:T(8,128)} async-done(((f32[512,512]{1,0:T(8,128)}), f32[512,512]{1,0:T(8,128)}) %all-reduce.2.cloned.1.call-update) | async-done | bytes 1048592 | tf_op jit(solution)/shard_map/psum | solution.py:20
  541.0 0.0 copy-done
  541.0 0.0 copy-start.1
  541.0 2.5 fusion.2
  543.5 0.3 fusion.16
  543.7 0.1 copy.8
  543.8 5.8 cholesky.44
  549.7 0.6 compare_reduce_fusion.1
  550.4 0.7 fusion.6
  551.0 4.9 custom-call.6
  555.9 0.3 convolution_bitcast_fusion.3
  556.3 0.0 copy-done.1
  556.3 1.2 fusion
  557.4 0.3 fusion.17
  557.7 0.1 copy.9
  557.8 5.8 cholesky.55
  563.7 0.6 compare_reduce_fusion
  564.3 0.7 fusion.7
  565.0 4.9 custom-call.7
  569.9 0.3 convolution_bitcast_fusion.2
  570.2 1.4 convolution_bitcast_fusion.1
  571.6 0.2 copy.10
  571.8 10.6 %all_to_all.37 = f32[2,4,64,128]{3,1,0,2:T(4,128)S(1)} all-to-all(f32[2,4,64,128]{3,1,0,2:T(4,128)S(1)} %copy.10), channel_id=1, replica_groups=mesh['gx'=8,'yz'=32,'ta'=2] {'gx'}, dimensions={2} | all-to-all | bytes 524288 | tf_op jit(solution)/shard_map/all_to_all | solution.py:29
  582.4 0.8 copy.15
  (4 shorter events, 0.1 us)
Async XLA Ops:
  6.5 534.5 %copy-start = (f32[512,64]{0,1:T(8,128)S(1)}, f32[512,64]{0,1:T(8,128)}, u32[]{:S(2)}) copy-start(f32[512,64]{0,1:T(8,128)} %param.6) | copy-start | bytes 393220
  6.5 534.5 %all-reduce.2.cloned.1.call-start = ((), (), s32[]{:S(2)}) async-start(), calls=%async_computation.2 | async-start | bytes 2097152 | tf_op jit(solution)/shard_map/psum | solution.py:20
  541.0 15.3 %copy-start.1 = (f32[512,512]{1,0:T(8,128)S(1)}, f32[512,512]{1,0:T(8,128)}, u32[]{:S(2)}) copy-start(f32[512,512]{1,0:T(8,128)} %all-reduce.2.cloned.1.call-done) | copy-start | bytes 3145732
Sparse Core Ops, SparseCore 0:
  75.6 465.3 all-reduce.1
where the time goes:
time: 590 us
  waiting for transfers between devices  466 us (79%)
  blocking collectives  47.1 us (8%)
  other arithmetic  31.4 us (5%)
  local copies, waits for them, and re-layouts  21.7 us (4%)
  between operations  13.5 us (2%)
  matrix products  10.8 us (2%)
    psum x1, waiting for transfers between devices, shards(): gram = lax.psum(partial_gram, ('gx', 'yz', 'ta'))  466 us
    all_to_all x1, blocking collectives, shards(): wide = lax.all_to_all(field, 'gx', split_axis=3, concat_axis=2, tiled=True)  36.5 us
    unnamed x7, local copies, waits for them, and re-layouts  16.4 us
    another operation x6, other arithmetic, orthonormal(): lower = jnp.linalg.cholesky(small)  13 us
  transfers between devices with their start and end apart: 1, of which 1 were waited for; matrix products, arithmetic and copies ran while one was open for 0% of the time, Pallas kernels for 0%

commit v1 on v0

v1 whole, which is shorter than its diff:
```python
import functools

import jax
import jax.numpy as jnp
from jax import lax
from jax.experimental import pallas as pl
from jax.experimental.pallas import tpu as pltpu
from jax.sharding import Mesh, PartitionSpec as P

ITERS = 2
LANES = 128
VMEM = pl.BlockSpec(memory_space=pltpu.VMEM)


def split(x):
    high = x.astype(jnp.bfloat16)
    return high, (x - high.astype(jnp.float32)).astype(jnp.bfloat16)


def pack_kernel(field_ref, out_ref):
    out_ref[0] = field_ref[...]


def pack(field, groups):
    moments, rows, _ = field.shape
    return pl.pallas_call(
        pack_kernel,
        grid=(groups,),
        in_specs=[pl.BlockSpec((moments, rows, LANES), lambda g: (0, 0, g))],
        out_specs=pl.BlockSpec((1, moments, rows, LANES), lambda g: (g, 0, 0, 0)),
        out_shape=jax.ShapeDtypeStruct((groups, moments, rows, LANES), jnp.float32),
    )(field)


def columns(wide_ref):
    groups, moments, rows, _ = wide_ref.shape
    return jnp.concatenate(
        [wide_ref[:, m].reshape(groups * rows, LANES) for m in range(moments)], axis=1
    )


def blocks(order):
    count = order // LANES
    return [(i, j) for i in range(count) for j in range(i, count)]


def gram_kernel(scale, wide_ref, out_ref):
    high, low = split(columns(wide_ref))
    order = high.shape[0]
    half = order // 2
    dims = (((1,), (1,)), ((), ()))
    dot = functools.partial(lax.dot_general, dimension_numbers=dims, preferred_element_type=jnp.float32)
    parts = {}
    for i in range(2):
        for j in range(i, 2):
            a, b = slice(i * half, (i + 1) * half), slice(j * half, (j + 1) * half)
            parts[i, j] = dot(high[a], high[b]) + (dot(high[a], low[b]) + dot(low[a], high[b]))
    per = half // LANES
    for place, (i, j) in enumerate(blocks(order)):
        part = parts[i // per, j // per]
        r, c = (i % per) * LANES, (j % per) * LANES
        out_ref[place * LANES : (place + 1) * LANES, :] = part[r : r + LANES, c : c + LANES] * scale


def inverse_factor(small):
    n = small.shape[0]
    row = lax.broadcasted_iota(jnp.int32, (n, n), 0)
    lane = lax.broadcasted_iota(jnp.int32, (n, n), 1)
    eye = (row == lane).astype(jnp.float32)
    work = jnp.concatenate([small, eye], axis=1)
    tiles = [work[8 * k : 8 * k + 8] for k in range(n // 8)]
    sub = lax.broadcasted_iota(jnp.int32, (8, 2 * n), 0)
    for j in range(n):
        k0, s = divmod(j, 8)
        pivot_row = jnp.broadcast_to(tiles[k0][s : s + 1, :], (8, 2 * n))
        inverse = 1.0 / jnp.broadcast_to(tiles[k0][s : s + 1, j : j + 1], (8, 2 * n))
        scaled = pivot_row * inverse
        for k in range(k0, n // 8):
            factor = jnp.broadcast_to(tiles[k][:, j : j + 1], (8, 2 * n))
            if k == k0:
                factor = jnp.where(sub > s, factor, 0.0)
            tiles[k] = tiles[k] - factor * scaled
    work = jnp.concatenate(tiles, axis=0)
    pivots = jnp.sum(jnp.where(row == lane, work[:, :n], 0.0), axis=1, keepdims=True)
    return work[:, n:] * lax.rsqrt(pivots)


def core_kernel(gram_ref, start_ref, wide_ref, out_ref, full_ref):
    order = full_ref.shape[0]
    for place, (i, j) in enumerate(blocks(order)):
        block = gram_ref[place * LANES : (place + 1) * LANES, :]
        full_ref[i * LANES : (i + 1) * LANES, j * LANES : (j + 1) * LANES] = block
        if i != j:
            full_ref[j * LANES : (j + 1) * LANES, i * LANES : (i + 1) * LANES] = block.T
    dot = functools.partial(jnp.dot, precision=lax.Precision.HIGHEST, preferred_element_type=jnp.float32)
    basis = start_ref[...]
    for step in range(ITERS):
        image = dot(basis, full_ref[...])
        small = lax.dot_general(
            image,
            image,
            (((1,), (1,)), ((), ())),
            precision=lax.Precision.HIGHEST,
            preferred_element_type=jnp.float32,
        )
        basis = dot(inverse_factor(small), image)
    high, low = split(basis)
    groups, moments, rows, _ = wide_ref.shape
    share = out_ref.shape[2]
    for m in range(moments):
        part_high, part_low = split(wide_ref[:, m].reshape(groups * rows, LANES))
        two = functools.partial(jnp.dot, preferred_element_type=jnp.float32)
        core = two(high, part_high) + (two(high, part_low) + two(low, part_high))
        out_ref[:, m] = core.reshape(groups, share, LANES)


def exchange(x, axes):
    return lax.all_to_all(x, axes, 0, 0, tiled=True)


def shards(count, group_axes, plane_axes, line_axes, field, start):
    groups = lax.axis_size(group_axes)
    flat = lax.axis_size(plane_axes)
    line = lax.axis_size(line_axes)
    times, species, rows, planes = field.shape
    moments = times * species
    order, rank = start.shape
    params = pltpu.CompilerParams(vmem_limit_bytes=40 * 1024 * 1024)

    packed = pack(field.reshape(moments, rows, planes), groups)
    wide = exchange(packed, group_axes)

    depth = len(blocks(order)) * LANES
    partial_gram = pl.pallas_call(
        functools.partial(gram_kernel, 1.0 / count),
        in_specs=[VMEM],
        out_specs=VMEM,
        out_shape=jax.ShapeDtypeStruct((depth, LANES), jnp.float32),
        compiler_params=params,
    )(wide)

    share = depth // flat
    pieces = exchange(partial_gram.reshape(flat, share, LANES), plane_axes)
    mine = jnp.sum(pieces, axis=0)
    mine = jnp.sum(exchange(jnp.broadcast_to(mine, (line, share, LANES)), line_axes), axis=0)
    gram = exchange(jnp.broadcast_to(mine, (flat, share, LANES)), plane_axes).reshape(depth, LANES)

    plane_core = pl.pallas_call(
        core_kernel,
        in_specs=[VMEM] * 3,
        out_specs=VMEM,
        out_shape=jax.ShapeDtypeStruct((groups, moments, rank // groups, LANES), jnp.float32),
        scratch_shapes=[pltpu.VMEM((order, order), jnp.float32)],
        compiler_params=params,
    )(gram, start.T, wide)
    core = exchange(plane_core, group_axes)
    core = jnp.transpose(core, (1, 2, 0, 3))
    return core.reshape(times, species, rank // groups, planes)


def solution(mesh):
    fine = Mesh(
        mesh.devices.reshape(4, 2, 8, 4, 2), ("y", "core", "z_lo", "x", "z_hi")
    )
    placed = P("z_hi", None, ("y", "core"), ("z_lo", "x"))

    def program(field, start):
        count = field.shape[0] * field.shape[1] * field.shape[3]
        body = functools.partial(
            shards, count, ("y", "core"), ("y", "core", "x"), ("z_lo", "z_hi")
        )
        return jax.shard_map(
            body, mesh=fine, in_specs=(placed, P()), out_specs=placed, check_vma=False
        )(field, start)

    return program
```

time: 590 us -> 144 us (0.24)
  waiting for transfers between devices: 466 us -> 0 us
  blocking collectives: 47.1 us -> 114 us
  other arithmetic: 31.4 us -> 0.08 us
  Pallas kernels: 0 us -> 27 us
  local copies, waits for them, and re-layouts: 21.7 us -> 0.98 us
  between operations: 13.5 us -> 0.03 us
  matrix products: 10.8 us -> 0 us
    psum x1 -> x0, waiting for transfers between devices: 466 us -> none  [shards(): gram = lax.psum(partial_gram, ('gx', 'yz', 'ta'))]
    all_to_all x2 -> x5, blocking collectives: 47.1 us -> 114 us  [exchange(): return lax.all_to_all(x, axes, 0, 0, tiled=True)]
    pallas_call x0 -> x3, Pallas kernels: none -> 27 us  [the longest x1 19.9 us: shards(): pl.pallas_call(core_kernel, in_specs=[VMEM] * 3, out_specs=VMEM, out_shap...]
    another operation x10 -> x0, other arithmetic: 24.1 us -> none  [the longest x6 13 us: orthonormal(): lower = jnp.linalg.cholesky(small)]
    unnamed x7 -> x2, local copies, waits for them, and re-layouts: 16.4 us -> 0.01 us
    dot_general x6 -> x0, matrix products: 10.1 us -> none  [the longest x1 4.56 us: shards(): lax.dot_general(wide, wide, (((0, 1, 3), (0, 1, 3)), ((), ())), precision...]
    all_to_all x1 -> x0, other arithmetic: 7.22 us -> none  [shards(): wide = lax.all_to_all(field, 'gx', split_axis=3, concat_axis=2, tiled=True)]
  transfers between devices with their start and end apart: 1 -> 0, of which waited for: 1 -> 0; matrix products, arithmetic and copies ran while one was open for 0% -> 0% of each run, Pallas kernels for 0% -> 0%
where the time goes in v1:
time: 144 us; the launch traced here: 142 us
  blocking collectives  114 us (79%)
  Pallas kernels  27 us (19%)
    all_to_all x5, blocking collectives, exchange(): return lax.all_to_all(x, axes, 0, 0, tiled=True)  114 us
    pallas_call x1, Pallas kernels, shards(): pl.pallas_call(core_kernel, in_specs=[VMEM] * 3, out_specs=VMEM, out_shap...  19.9 us
    pallas_call x1, Pallas kernels, pack(): pl.pallas_call(pack_kernel, grid=(groups,), in_specs=[pl.BlockSpec((momen...  5.65 us

profile of v1, /device:TPU:1, one launch (start us, length us, event | category | flops | bytes accessed | tf_op | source)
XLA Modules:
  0.0 142.1 jit_solution(3563220328794216013)
XLA Ops:
  0.0 5.6 %shard_map.28 = f32[8,8,64,128]{3,2,1,0:T(8,128)} custom-call(f32[8,64,1024]{2,1,0:T(8,128)} %bitcast.10), custom_call_target="tpu_custom_call" | custom-call | tf_op jit(solution)/shard_map/pallas_call | solution.py:26
  5.7 36.9 %all_to_all.25.wide_ref = f32[8,8,64,128]{3,2,1,0:T(8,128)S(1)} all-to-all(f32[8,8,64,128]{3,2,1,0:T(8,128)} %shard_map.28), channel_id=1, replica_groups=mesh['y'=4,'core'=2,'z_lo'=8,'x'=4,'z_hi'=2] {'y','core'}, dimensions={0} | all-to-all | bytes 4194304 | tf_op jit(solution)/shard_map/all_to_all | solution.py:118
  42.5 1.4 %shard_map.29 = f32[1280,128]{1,0:T(8,128)S(1)} custom-call(f32[8,8,64,128]{3,2,1,0:T(8,128)S(1)} %all_to_all.25.wide_ref), custom_call_target="tpu_custom_call" | custom-call | tf_op jit(solution)/shard_map/pallas_call | solution.py:134
  43.9 16.3 %all_to_all.26 = f32[32,40,128]{2,1,0:T(8,128)S(1)} all-to-all(f32[32,40,128]{2,1,0:T(8,128)S(1)} %bitcast.8), channel_id=1, replica_groups=mesh['y'=4,'core'=2,'z_lo'=8,'x'=4,'z_hi'=2] {'y','core','x'}, dimensions={0} | all-to-all | bytes 1310720 | tf_op jit(solution)/shard_map/all_to_all | solution.py:118
  60.3 0.0 copy-start
  60.3 0.1 reduce_sum.18
  60.4 29.4 %all_to_all.27 = f32[16,40,128]{2,1,0:T(8,128)S(1)} all-to-all(f32[16,40,128]{2,1,0:T(8,128)S(1)} %broadcast_in_dim.6), channel_id=1, replica_groups=mesh['y'=4,'core'=2,'z_lo'=8,'x'=4,'z_hi'=2] {'z_lo','z_hi'}, dimensions={0} | all-to-all | bytes 655360 | tf_op jit(solution)/shard_map/all_to_all | solution.py:118
  89.8 21.7 %all_to_all.28 = f32[32,40,128]{2,1,0:T(8,128)S(1)} all-to-all(f32[32,40,128]{2,1,0:T(8,128)S(1)} %broadcast_in_dim.7), channel_id=1, replica_groups=mesh['y'=4,'core'=2,'z_lo'=8,'x'=4,'z_hi'=2] {'y','core','x'}, dimensions={0} | all-to-all | bytes 1310720 | tf_op jit(solution)/shard_map/all_to_all | solution.py:118
  111.5 0.0 copy-done
  111.5 19.9 %shard_map.30 = f32[8,8,8,128]{3,2,1,0:T(8,128)S(1)} custom-call(f32[1280,128]{1,0:T(8,128)S(1)} %bitcast.7, f32[64,512]{1,0:T(8,128)S(1)} %bitcast.9, f32[8,8,64,128]{3,2,1,0:T(8,128)S(1)} %all_to_all.25.wide_ref), custom_call_target="tpu_custom_call" | custom-call | tf_op jit(solution)/shard_map/pallas_call | solution.py:148
  131.4 9.8 %all_to_all.29 = f32[8,8,8,128]{3,2,1,0:T(8,128)S(1)} all-to-all(f32[8,8,8,128]{3,2,1,0:T(8,128)S(1)} %shard_map.30), channel_id=1, replica_groups=mesh['y'=4,'core'=2,'z_lo'=8,'x'=4,'z_hi'=2] {'y','core'}, dimensions={0} | all-to-all | bytes 524288 | tf_op jit(solution)/shard_map/all_to_all | solution.py:118
  141.2 0.2 copy.4
  141.4 0.7 reshape.15
  (3 shorter events, 0.1 us)
Async XLA Ops:
  60.3 51.2 %copy-start = (f32[512,64]{0,1:T(8,128)S(1)}, f32[512,64]{0,1:T(8,128)}, u32[]{:S(2)}) copy-start(f32[512,64]{0,1:T(8,128)} %param.3) | copy-start | bytes 393220

commit v2 on v1

--- a/solution.py
+++ b/solution.py
@@ -15,21 +15,6 @@
 def split(x):
     high = x.astype(jnp.bfloat16)
     return high, (x - high.astype(jnp.float32)).astype(jnp.bfloat16)
-
-
-def pack_kernel(field_ref, out_ref):
-    out_ref[0] = field_ref[...]
-
-
-def pack(field, groups):
-    moments, rows, _ = field.shape
-    return pl.pallas_call(
-        pack_kernel,
-        grid=(groups,),
-        in_specs=[pl.BlockSpec((moments, rows, LANES), lambda g: (0, 0, g))],
-        out_specs=pl.BlockSpec((1, moments, rows, LANES), lambda g: (g, 0, 0, 0)),
-        out_shape=jax.ShapeDtypeStruct((groups, moments, rows, LANES), jnp.float32),
-    )(field)
 
 
 def columns(wide_ref):
@@ -62,27 +47,47 @@
         out_ref[place * LANES : (place + 1) * LANES, :] = part[r : r + LANES, c : c + LANES] * scale
 
 
-def inverse_factor(small):
-    n = small.shape[0]
-    row = lax.broadcasted_iota(jnp.int32, (n, n), 0)
-    lane = lax.broadcasted_iota(jnp.int32, (n, n), 1)
-    eye = (row == lane).astype(jnp.float32)
-    work = jnp.concatenate([small, eye], axis=1)
-    tiles = [work[8 * k : 8 * k + 8] for k in range(n // 8)]
-    sub = lax.broadcasted_iota(jnp.int32, (8, 2 * n), 0)
-    for j in range(n):
-        k0, s = divmod(j, 8)
-        pivot_row = jnp.broadcast_to(tiles[k0][s : s + 1, :], (8, 2 * n))
-        inverse = 1.0 / jnp.broadcast_to(tiles[k0][s : s + 1, j : j + 1], (8, 2 * n))
-        scaled = pivot_row * inverse
-        for k in range(k0, n // 8):
-            factor = jnp.broadcast_to(tiles[k][:, j : j + 1], (8, 2 * n))
-            if k == k0:
-                factor = jnp.where(sub > s, factor, 0.0)
-            tiles[k] = tiles[k] - factor * scaled
-    work = jnp.concatenate(tiles, axis=0)
-    pivots = jnp.sum(jnp.where(row == lane, work[:, :n], 0.0), axis=1, keepdims=True)
-    return work[:, n:] * lax.rsqrt(pivots)
+def inverse_factor(work):
+    n = work.shape[0]
+    shape = (8, 2 * n)
+    panels = n // 8
+    tiles = [work[8 * k : 8 * k + 8] for k in range(panels)]
+    sub = lax.broadcasted_iota(jnp.int32, shape, 0)
+    done = []
+    for p in range(panels):
+        at = n + 8 * p
+        columns_of = [jnp.broadcast_to(tiles[p][:, at + j : at + j + 1], shape) for j in range(8)]
+        rows = [jnp.broadcast_to(tiles[p][i : i + 1], shape) for i in range(8)]
+        pivot = {
+            (i, j): jnp.broadcast_to(columns_of[j][i : i + 1], shape) for j in range(8) for i in range(j, 8)
+        }
+        factor, inverse = {}, []
+        for i in range(8):
+            inverse.append(1.0 / pivot[i, i])
+            for j in range(i + 1, 8):
+                factor[j, i] = pivot[j, i] * inverse[i]
+            for j in range(i + 1, 8):
+                for m in range(i + 1, j + 1):
+                    pivot[j, m] = pivot[j, m] - factor[j, i] * pivot[m, i]
+                rows[j] = rows[j] - factor[j, i] * rows[i]
+        final = rows[0] * lax.rsqrt(pivot[0, 0])
+        for i in range(1, 8):
+            final = jnp.where(sub == i, rows[i] * lax.rsqrt(pivot[i, i]), final)
+        done.append(final)
+        solved = [None] * 8
+        for i in range(7, -1, -1):
+            value = rows[i] * inverse[i]
+            for k in range(i + 1, 8):
+                value = value - factor[k, i] * solved[k]
+            solved[i] = value
+        for t in range(p + 1, panels):
+            terms = [
+                jnp.broadcast_to(tiles[t][:, at + j : at + j + 1], shape) * solved[j] for j in range(8)
+            ]
+            while len(terms) > 1:
+                terms = [x + y for x, y in zip(terms[::2], terms[1::2])]
+            tiles[t] = tiles[t] - terms[0]
+    return jnp.concatenate(done, axis=0)[:, :n]
 
 
 def core_kernel(gram_ref, start_ref, wide_ref, out_ref, full_ref):
@@ -94,16 +99,20 @@
             full_ref[j * LANES : (j + 1) * LANES, i * LANES : (i + 1) * LANES] = block.T
     dot = functools.partial(jnp.dot, precision=lax.Precision.HIGHEST, preferred_element_type=jnp.float32)
     basis = start_ref[...]
+    rank = basis.shape[0]
+    shape = (rank, 2 * rank)
+    row, lane = (lax.broadcasted_iota(jnp.int32, shape, axis) for axis in (0, 1))
+    eye = (row == lane).astype(jnp.float32)
     for step in range(ITERS):
         image = dot(basis, full_ref[...])
         small = lax.dot_general(
             image,
-            image,
+            jnp.concatenate([jnp.zeros_like(image), image], axis=0),
             (((1,), (1,)), ((), ())),
             precision=lax.Precision.HIGHEST,
             preferred_element_type=jnp.float32,
         )
-        basis = dot(inverse_factor(small), image)
+        basis = dot(inverse_factor(small + eye), image)
     high, low = split(basis)
     groups, moments, rows, _ = wide_ref.shape
     share = out_ref.shape[2]
@@ -121,13 +130,13 @@
 def shards(count, group_axes, plane_axes, line_axes, field, start):
     groups = lax.axis_size(group_axes)
     flat = lax.axis_size(plane_axes)
-    line = lax.axis_size(line_axes)
     times, species, rows, planes = field.shape
     moments = times * species
     order, rank = start.shape
     params = pltpu.CompilerParams(vmem_limit_bytes=40 * 1024 * 1024)
 
-    packed = pack(field.reshape(moments, rows, planes), groups)
+    tiles = field.reshape(moments, rows // 8, 8, groups, LANES)
+    packed = jnp.transpose(tiles, (3, 0, 1, 2, 4)).reshape(groups, moments, rows, LANES)
     wide = exchange(packed, group_axes)
 
     depth = len(blocks(order)) * LANES
@@ -142,7 +151,9 @@
     share = depth // flat
     pieces = exchange(partial_gram.reshape(flat, share, LANES), plane_axes)
     mine = jnp.sum(pieces, axis=0)
-    mine = jnp.sum(exchange(jnp.broadcast_to(mine, (line, share, LANES)), line_axes), axis=0)
+    for axes in line_axes:
+        spread = jnp.broadcast_to(mine, (lax.axis_size(axes), share, LANES))
+        mine = jnp.sum(exchange(spread, axes), axis=0)
     gram = exchange(jnp.broadcast_to(mine, (flat, share, LANES)), plane_axes).reshape(depth, LANES)
 
     plane_core = pl.pallas_call(
@@ -160,14 +171,14 @@
 
 def solution(mesh):
     fine = Mesh(
-        mesh.devices.reshape(4, 2, 8, 4, 2), ("y", "core", "z_lo", "x", "z_hi")
+        mesh.devices.reshape(4, 2, 2, 4, 4, 2), ("y", "core", "z_mid", "z_near", "x", "z_hi")
     )
-    placed = P("z_hi", None, ("y", "core"), ("z_lo", "x"))
+    placed = P("z_hi", None, ("y", "core"), ("z_mid", "z_near", "x"))
 
     def program(field, start):
         count = field.shape[0] * field.shape[1] * field.shape[3]
         body = functools.partial(
-            shards, count, ("y", "core"), ("y", "core", "x"), ("z_lo", "z_hi")
+            shards, count, ("y", "core"), ("y", "core", "x"), ("z_near", ("z_mid", "z_hi"))
         )
         return jax.shard_map(
             body, mesh=fine, in_specs=(placed, P()), out_specs=placed, check_vma=False

time: 144 us -> 127 us (0.88)
  Pallas kernels: 27 us -> 9.54 us
  local copies, waits for them, and re-layouts: 0.98 us -> 2.83 us
    pallas_call x1, Pallas kernels: 19.9 us -> 8.11 us  [shards(): pl.pallas_call(core_kernel, in_specs=[VMEM] * 3, out_specs=VMEM, out_shap...]
    pallas_call x1 -> x0, Pallas kernels: 5.65 us -> none  [pack(): pl.pallas_call(pack_kernel, grid=(groups,), in_specs=[pl.BlockSpec((momen...]
    reshape x0 -> x1, local copies, waits for them, and re-layouts: none -> 1.86 us  [shards(): tiles = field.reshape(moments, rows // 8, 8, groups, LANES)]
    all_to_all x5 -> x6, blocking collectives: 114 us -> 114 us  [exchange(): return lax.all_to_all(x, axes, 0, 0, tiled=True)]
where the time goes in v2:
time: 127 us; the launch traced here: 126 us
  blocking collectives  114 us (90%)
  Pallas kernels  9.54 us (8%)
  local copies, waits for them, and re-layouts  2.83 us (2%)
    all_to_all x6, blocking collectives, exchange(): return lax.all_to_all(x, axes, 0, 0, tiled=True)  114 us
    pallas_call x1, Pallas kernels, shards(): pl.pallas_call(core_kernel, in_specs=[VMEM] * 3, out_specs=VMEM, out_shap...  8.11 us

profile of v2, /device:TPU:1, one launch (start us, length us, event | category | flops | bytes accessed | tf_op | source)
XLA Modules:
  0.0 126.5 jit_solution(17619049949948061139)
XLA Ops:
  0.0 1.9 %copy.9 = f32[8,8,8,8,128]{4,2,1,0,3:T(8,128)S(1)} copy(f32[8,8,8,8,128]{4,2,3,1,0:T(8,128)} %bitcast.16) | data formatting | bytes 4194304 | tf_op jit(solution)/shard_map/reshape | solution.py:138
  1.9 35.8 %all_to_all.30.wide_ref = f32[8,8,64,128]{3,2,1,0:T(8,128)S(1)} all-to-all(f32[8,8,64,128]{3,2,1,0:T(8,128)S(1)} %bitcast.15), channel_id=1, replica_groups=mesh['y'=4,'core'=2,'z_mid'=2,'z_near'=4,'x'=4,'z_hi'=2] {'y','core'}, dimensions={0} | all-to-all | bytes 4194304 | tf_op jit(solution)/shard_map/all_to_all | solution.py:127
  37.7 1.4 %shard_map.28 = f32[1280,128]{1,0:T(8,128)S(1)} custom-call(f32[8,8,64,128]{3,2,1,0:T(8,128)S(1)} %all_to_all.30.wide_ref), custom_call_target="tpu_custom_call" | custom-call | tf_op jit(solution)/shard_map/pallas_call | solution.py:143
  39.1 0.0 copy-start
  39.1 16.5 %all_to_all.31 = f32[32,40,128]{2,1,0:T(8,128)S(1)} all-to-all(f32[32,40,128]{2,1,0:T(8,128)S(1)} %bitcast.13), channel_id=1, replica_groups=mesh['y'=4,'core'=2,'z_mid'=2,'z_near'=4,'x'=4,'z_hi'=2] {'y','core','x'}, dimensions={0} | all-to-all | bytes 1310720 | tf_op jit(solution)/shard_map/all_to_all | solution.py:127
  55.6 0.1 reduce_sum.27
  55.6 8.6 %all_to_all.32 = f32[4,40,128]{2,1,0:T(8,128)S(1)} all-to-all(f32[4,40,128]{2,1,0:T(8,128)S(1)} %broadcast_in_dim.9), channel_id=1, replica_groups=mesh['y'=4,'core'=2,'z_mid'=2,'z_near'=4,'x'=4,'z_hi'=2] {'z_near'}, dimensions={0} | all-to-all | bytes 163840 | tf_op jit(solution)/shard_map/all_to_all | solution.py:127
  64.2 23.7 %all_to_all.33 = f32[4,40,128]{2,1,0:T(8,128)S(1)} all-to-all(f32[4,40,128]{2,1,0:T(8,128)S(1)} %broadcast_in_dim.10), channel_id=1, replica_groups=mesh['y'=4,'core'=2,'z_mid'=2,'z_near'=4,'x'=4,'z_hi'=2] {'z_mid','z_hi'}, dimensions={0} | all-to-all | bytes 163840 | tf_op jit(solution)/shard_map/all_to_all | solution.py:127
  88.0 19.6 %all_to_all.34 = f32[32,40,128]{2,1,0:T(8,128)S(1)} all-to-all(f32[32,40,128]{2,1,0:T(8,128)S(1)} %broadcast_in_dim.11), channel_id=1, replica_groups=mesh['y'=4,'core'=2,'z_mid'=2,'z_near'=4,'x'=4,'z_hi'=2] {'y','core','x'}, dimensions={0} | all-to-all | bytes 1310720 | tf_op jit(solution)/shard_map/all_to_all | solution.py:127
  107.6 0.0 copy-done
  107.6 8.1 %shard_map.29 = f32[8,8,8,128]{3,2,1,0:T(8,128)S(1)} custom-call(f32[1280,128]{1,0:T(8,128)S(1)} %bitcast.12, f32[64,512]{1,0:T(8,128)S(1)} %bitcast.14, f32[8,8,64,128]{3,2,1,0:T(8,128)S(1)} %all_to_all.30.wide_ref), custom_call_target="tpu_custom_call" | custom-call | tf_op jit(solution)/shard_map/pallas_call | solution.py:159
  115.7 9.8 %all_to_all.35 = f32[8,8,8,128]{3,2,1,0:T(8,128)S(1)} all-to-all(f32[8,8,8,128]{3,2,1,0:T(8,128)S(1)} %shard_map.29), channel_id=1, replica_groups=mesh['y'=4,'core'=2,'z_mid'=2,'z_near'=4,'x'=4,'z_hi'=2] {'y','core'}, dimensions={0} | all-to-all | bytes 524288 | tf_op jit(solution)/shard_map/all_to_all | solution.py:127
  125.6 0.2 copy.7
  125.7 0.7 reshape.19
  (5 shorter events, 0.1 us)
Async XLA Ops:
  39.1 68.5 %copy-start = (f32[512,64]{0,1:T(8,128)S(1)}, f32[512,64]{0,1:T(8,128)}, u32[]{:S(2)}) copy-start(f32[512,64]{0,1:T(8,128)} %param.3) | copy-start | bytes 393220

commit v3 on v2

--- a/solution.py
+++ b/solution.py
@@ -9,6 +9,7 @@
 
 ITERS = 2
 LANES = 128
+SLAB = 4
 VMEM = pl.BlockSpec(memory_space=pltpu.VMEM)
 
 
@@ -127,9 +128,19 @@
     return lax.all_to_all(x, axes, 0, 0, tiled=True)
 
 
+def added(pieces, count):
+    return jnp.sum(pieces.reshape(count, pieces.shape[0] // count, *pieces.shape[1:]), axis=0)
+
+
+def spread(block, count):
+    copies = jnp.broadcast_to(block, (count, *block.shape))
+    return copies.reshape(count * block.shape[0], *block.shape[1:])
+
+
 def shards(count, group_axes, plane_axes, line_axes, field, start):
     groups = lax.axis_size(group_axes)
     flat = lax.axis_size(plane_axes)
+    line = lax.axis_size(line_axes)
     times, species, rows, planes = field.shape
     moments = times * species
     order, rank = start.shape
@@ -148,13 +159,11 @@
         compiler_params=params,
     )(wide)
 
-    share = depth // flat
-    pieces = exchange(partial_gram.reshape(flat, share, LANES), plane_axes)
-    mine = jnp.sum(pieces, axis=0)
-    for axes in line_axes:
-        spread = jnp.broadcast_to(mine, (lax.axis_size(axes), share, LANES))
-        mine = jnp.sum(exchange(spread, axes), axis=0)
-    gram = exchange(jnp.broadcast_to(mine, (flat, share, LANES)), plane_axes).reshape(depth, LANES)
+    share = depth // flat // SLAB
+    pieces = exchange(partial_gram.reshape(flat * share, SLAB, LANES), plane_axes)
+    mine = added(pieces, flat)
+    mine = added(exchange(spread(mine, line), line_axes), line)
+    gram = exchange(spread(mine, flat), plane_axes).reshape(depth, LANES)
 
     plane_core = pl.pallas_call(
         core_kernel,
@@ -171,14 +180,14 @@
 
 def solution(mesh):
     fine = Mesh(
-        mesh.devices.reshape(4, 2, 2, 4, 4, 2), ("y", "core", "z_mid", "z_near", "x", "z_hi")
+        mesh.devices.reshape(4, 2, 4, 2, 4, 2), ("y", "core", "z_mid", "z_pair", "x", "z_hi")
     )
-    placed = P("z_hi", None, ("y", "core"), ("z_mid", "z_near", "x"))
+    placed = P("z_hi", None, ("y", "core"), ("z_mid", "z_pair", "x"))
 
     def program(field, start):
         count = field.shape[0] * field.shape[1] * field.shape[3]
         body = functools.partial(
-            shards, count, ("y", "core"), ("y", "core", "x"), ("z_near", ("z_mid", "z_hi"))
+            shards, count, ("y", "core"), ("y", "core", "z_pair", "x"), ("z_mid", "z_hi")
         )
         return jax.shard_map(
             body, mesh=fine, in_specs=(placed, P()), out_specs=placed, check_vma=False

time: 127 us -> 121 us (0.953)
  blocking collectives: 114 us -> 108 us
    all_to_all x6 -> x5, blocking collectives: 114 us -> 108 us  [exchange(): return lax.all_to_all(x, axes, 0, 0, tiled=True)]
where the time goes in v3:
time: 121 us
  blocking collectives  108 us (89%)
  Pallas kernels  9.54 us (8%)
  local copies, waits for them, and re-layouts  2.87 us (2%)
    all_to_all x5, blocking collectives, exchange(): return lax.all_to_all(x, axes, 0, 0, tiled=True)  108 us
    pallas_call x1, Pallas kernels, shards(): pl.pallas_call(core_kernel, in_specs=[VMEM] * 3, out_specs=VMEM, out_shap...  8.11 us

profile of v3, /device:TPU:1, one launch (start us, length us, event | category | flops | bytes accessed | tf_op | source)
XLA Modules:
  0.0 120.8 jit_solution(11388996897126190062)
XLA Ops:
  0.0 1.9 %copy.13 = f32[8,8,8,8,128]{4,2,1,0,3:T(8,128)S(1)} copy(f32[8,8,8,8,128]{4,2,3,1,0:T(8,128)} %bitcast.22) | data formatting | bytes 4194304 | tf_op jit(solution)/shard_map/reshape | solution.py:149
  1.9 35.8 %all_to_all.25.wide_ref = f32[8,8,64,128]{3,2,1,0:T(8,128)S(1)} all-to-all(f32[8,8,64,128]{3,2,1,0:T(8,128)S(1)} %bitcast.19), channel_id=1, replica_groups=mesh['y'=4,'core'=2,'z_mid'=4,'z_pair'=2,'x'=4,'z_hi'=2] {'y','core'}, dimensions={0} | all-to-all | bytes 4194304 | tf_op jit(solution)/shard_map/all_to_all | solution.py:128
  37.7 1.4 %shard_map.28 = f32[1280,128]{1,0:T(8,128)S(1)} custom-call(f32[8,8,64,128]{3,2,1,0:T(8,128)S(1)} %all_to_all.25.wide_ref), custom_call_target="tpu_custom_call" | custom-call | tf_op jit(solution)/shard_map/pallas_call | solution.py:154
  39.1 0.0 copy-start
  39.1 18.3 %all_to_all.26 = f32[320,4,128]{2,1,0:T(4,128)S(1)} all-to-all(f32[320,4,128]{2,1,0:T(4,128)S(1)} %bitcast.17), channel_id=1, replica_groups=mesh['y'=4,'core'=2,'z_mid'=4,'z_pair'=2,'x'=4,'z_hi'=2] {'y','core','z_..., dimensions={0} | all-to-all | bytes 1310720 | tf_op jit(solution)/shard_map/all_to_all | solution.py:128
  57.4 0.1 reduce_sum.18
  57.6 24.8 %all_to_all.27 = f32[40,4,128]{2,1,0:T(4,128)S(1)} all-to-all(f32[40,4,128]{2,1,0:T(4,128)S(1)} %bitcast.25), channel_id=1, replica_groups=mesh['y'=4,'core'=2,'z_mid'=4,'z_pair'=2,'x'=4,'z_hi'=2] {'z_mid','z_hi'}, dimensions={0} | all-to-all | bytes 163840 | tf_op jit(solution)/shard_map/all_to_all | solution.py:128
  82.5 0.1 broadcast_in_dim.7
  82.5 19.9 %all_to_all.28 = f32[320,4,128]{2,1,0:T(4,128)S(1)} all-to-all(f32[320,4,128]{2,1,0:T(4,128)S(1)} %bitcast.21), channel_id=1, replica_groups=mesh['y'=4,'core'=2,'z_mid'=4,'z_pair'=2,'x'=4,'z_hi'=2] {'y','core','z_..., dimensions={0} | all-to-all | bytes 1310720 | tf_op jit(solution)/shard_map/all_to_all | solution.py:128
  102.5 0.0 copy-done
  102.5 8.1 %shard_map.29 = f32[8,8,8,128]{3,2,1,0:T(8,128)S(1)} custom-call(f32[1280,128]{1,0:T(8,128)S(1)} %bitcast.16, f32[64,512]{1,0:T(8,128)S(1)} %bitcast.18, f32[8,8,64,128]{3,2,1,0:T(8,128)S(1)} %all_to_all.25.wide_ref), custom_call_target="tpu_custom_call" | custom-call | tf_op jit(solution)/shard_map/pallas_call | solution.py:168
  110.6 9.3 %all_to_all.29 = f32[8,8,8,128]{3,2,1,0:T(8,128)S(1)} all-to-all(f32[8,8,8,128]{3,2,1,0:T(8,128)S(1)} %shard_map.29), channel_id=1, replica_groups=mesh['y'=4,'core'=2,'z_mid'=4,'z_pair'=2,'x'=4,'z_hi'=2] {'y','core'}, dimensions={0} | all-to-all | bytes 524288 | tf_op jit(solution)/shard_map/all_to_all | solution.py:128
  119.9 0.2 copy.10
  120.0 0.7 reshape.35
  (2 shorter events, 0.0 us)
Async XLA Ops:
  39.1 63.4 %copy-start = (f32[512,64]{0,1:T(8,128)S(1)}, f32[512,64]{0,1:T(8,128)}, u32[]{:S(2)}) copy-start(f32[512,64]{0,1:T(8,128)} %param.3) | copy-start | bytes 393220

commit v4 on v3

--- a/solution.py
+++ b/solution.py
@@ -18,20 +18,13 @@
     return high, (x - high.astype(jnp.float32)).astype(jnp.bfloat16)
 
 
-def columns(wide_ref):
-    groups, moments, rows, _ = wide_ref.shape
-    return jnp.concatenate(
-        [wide_ref[:, m].reshape(groups * rows, LANES) for m in range(moments)], axis=1
-    )
-
-
 def blocks(order):
     count = order // LANES
     return [(i, j) for i in range(count) for j in range(i, count)]
 
 
 def gram_kernel(scale, wide_ref, out_ref):
-    high, low = split(columns(wide_ref))
+    high, low = split(wide_ref[...])
     order = high.shape[0]
     half = order // 2
     dims = (((1,), (1,)), ((), ()))
@@ -115,13 +108,9 @@
         )
         basis = dot(inverse_factor(small + eye), image)
     high, low = split(basis)
-    groups, moments, rows, _ = wide_ref.shape
-    share = out_ref.shape[2]
-    for m in range(moments):
-        part_high, part_low = split(wide_ref[:, m].reshape(groups * rows, LANES))
-        two = functools.partial(jnp.dot, preferred_element_type=jnp.float32)
-        core = two(high, part_high) + (two(high, part_low) + two(low, part_high))
-        out_ref[:, m] = core.reshape(groups, share, LANES)
+    part_high, part_low = split(wide_ref[...])
+    two = functools.partial(jnp.dot, preferred_element_type=jnp.float32)
+    out_ref[...] = two(high, part_high) + (two(high, part_low) + two(low, part_high))
 
 
 def exchange(x, axes):
@@ -146,9 +135,9 @@
     order, rank = start.shape
     params = pltpu.CompilerParams(vmem_limit_bytes=40 * 1024 * 1024)
 
-    tiles = field.reshape(moments, rows // 8, 8, groups, LANES)
-    packed = jnp.transpose(tiles, (3, 0, 1, 2, 4)).reshape(groups, moments, rows, LANES)
-    wide = exchange(packed, group_axes)
+    wide = exchange(field.reshape(moments, rows, planes), group_axes)
+    wide = wide.reshape(groups, moments // groups, rows, planes)
+    wide = jnp.moveaxis(wide, 1, 2).reshape(order, moments // groups * planes)
 
     depth = len(blocks(order)) * LANES
     partial_gram = pl.pallas_call(
@@ -169,12 +158,13 @@
         core_kernel,
         in_specs=[VMEM] * 3,
         out_specs=VMEM,
-        out_shape=jax.ShapeDtypeStruct((groups, moments, rank // groups, LANES), jnp.float32),
+        out_shape=jax.ShapeDtypeStruct((rank, wide.shape[1]), jnp.float32),
         scratch_shapes=[pltpu.VMEM((order, order), jnp.float32)],
         compiler_params=params,
     )(gram, start.T, wide)
-    core = exchange(plane_core, group_axes)
-    core = jnp.transpose(core, (1, 2, 0, 3))
+    plane_core = plane_core.reshape(rank, moments // groups, planes)
+    plane_core = plane_core.reshape(groups, rank // groups, moments // groups, planes)
+    core = exchange(jnp.moveaxis(plane_core, 2, 1).reshape(moments, rank // groups, planes), group_axes)
     return core.reshape(times, species, rank // groups, planes)
 
 

time: 121 us -> 119 us (0.983)
  local copies, waits for them, and re-layouts: 2.87 us -> 0.81 us
    reshape x2 -> x0, local copies, waits for them, and re-layouts: 2.6 us -> none  [the longest x1 1.86 us: shards(): tiles = field.reshape(moments, rows // 8, 8, groups, LANES)]
where the time goes in v4:
time: 119 us
  blocking collectives  108 us (91%)
  Pallas kernels  9.66 us (8%)
    all_to_all x5, blocking collectives, exchange(): return lax.all_to_all(x, axes, 0, 0, tiled=True)  108 us
    pallas_call x1, Pallas kernels, shards(): pl.pallas_call(core_kernel, in_specs=[VMEM] * 3, out_specs=VMEM, out_shap...  8.23 us

profile of v4, /device:TPU:1, one launch (start us, length us, event | category | flops | bytes accessed | tf_op | source)
XLA Modules:
  0.0 119.0 jit_solution(18251028210013514829)
XLA Ops:
  0.0 36.9 %all_to_all.25 = f32[8,64,1024]{2,1,0:T(8,128)S(1)} all-to-all(f32[8,64,1024]{2,1,0:T(8,128)} %bitcast.19), channel_id=1, replica_groups=mesh['y'=4,'core'=2,'z_mid'=4,'z_pair'=2,'x'=4,'z_hi'=2] {'y','core'}, dimensions={0} | all-to-all | bytes 4194304 | tf_op jit(solution)/shard_map/all_to_all | solution.py:117
  36.9 1.4 %shard_map.28 = f32[1280,128]{1,0:T(8,128)S(1)} custom-call(f32[512,1024]{1,0:T(8,128)S(1)} %bitcast.11), custom_call_target="tpu_custom_call" | custom-call | tf_op jit(solution)/shard_map/pallas_call | solution.py:143
  38.3 0.0 copy-start
  38.3 18.3 %all_to_all.26 = f32[320,4,128]{2,1,0:T(4,128)S(1)} all-to-all(f32[320,4,128]{2,1,0:T(4,128)S(1)} %bitcast.14), channel_id=1, replica_groups=mesh['y'=4,'core'=2,'z_mid'=4,'z_pair'=2,'x'=4,'z_hi'=2] {'y','core','z_..., dimensions={0} | all-to-all | bytes 1310720 | tf_op jit(solution)/shard_map/all_to_all | solution.py:117
  56.6 0.1 reduce_sum.18
  56.8 24.0 %all_to_all.27 = f32[40,4,128]{2,1,0:T(4,128)S(1)} all-to-all(f32[40,4,128]{2,1,0:T(4,128)S(1)} %bitcast.22), channel_id=1, replica_groups=mesh['y'=4,'core'=2,'z_mid'=4,'z_pair'=2,'x'=4,'z_hi'=2] {'z_mid','z_hi'}, dimensions={0} | all-to-all | bytes 163840 | tf_op jit(solution)/shard_map/all_to_all | solution.py:117
  80.8 0.1 broadcast_in_dim.7
  80.9 19.9 %all_to_all.28 = f32[320,4,128]{2,1,0:T(4,128)S(1)} all-to-all(f32[320,4,128]{2,1,0:T(4,128)S(1)} %bitcast.18), channel_id=1, replica_groups=mesh['y'=4,'core'=2,'z_mid'=4,'z_pair'=2,'x'=4,'z_hi'=2] {'y','core','z_..., dimensions={0} | all-to-all | bytes 1310720 | tf_op jit(solution)/shard_map/all_to_all | solution.py:117
  100.8 0.0 copy-done
  100.8 8.2 %shard_map.29 = f32[64,1024]{1,0:T(8,128)S(1)} custom-call(f32[1280,128]{1,0:T(8,128)S(1)} %bitcast.13, f32[64,512]{1,0:T(8,128)S(1)} %bitcast.16, f32[512,1024]{1,0:T(8,128)S(1)} %bitcast.12), custom_call_target="tpu_custom_call" | custom-call | tf_op jit(solution)/shard_map/pallas_call | solution.py:157
  109.1 9.2 %all_to_all.29 = f32[8,8,1024]{2,1,0:T(8,128)S(1)} all-to-all(f32[8,8,1024]{2,1,0:T(8,128)S(1)} %bitcast.15), channel_id=1, replica_groups=mesh['y'=4,'core'=2,'z_mid'=4,'z_pair'=2,'x'=4,'z_hi'=2] {'y','core'}, dimensions={0} | all-to-all | bytes 524288 | tf_op jit(solution)/shard_map/all_to_all | solution.py:117
  118.3 0.7 copy.6
  (2 shorter events, 0.0 us)
Async XLA Ops:
  38.3 62.5 %copy-start = (f32[512,64]{0,1:T(8,128)S(1)}, f32[512,64]{0,1:T(8,128)}, u32[]{:S(2)}) copy-start(f32[512,64]{0,1:T(8,128)} %param.3) | copy-start | bytes 393220

commit v5 on v4

--- a/solution.py
+++ b/solution.py
@@ -126,10 +126,8 @@
     return copies.reshape(count * block.shape[0], *block.shape[1:])
 
 
-def shards(count, group_axes, plane_axes, line_axes, field, start):
+def shards(count, group_axes, core_axes, plane_axes, line_axes, field, start):
     groups = lax.axis_size(group_axes)
-    flat = lax.axis_size(plane_axes)
-    line = lax.axis_size(line_axes)
     times, species, rows, planes = field.shape
     moments = times * species
     order, rank = start.shape
@@ -148,11 +146,14 @@
         compiler_params=params,
     )(wide)
 
-    share = depth // flat // SLAB
-    pieces = exchange(partial_gram.reshape(flat * share, SLAB, LANES), plane_axes)
-    mine = added(pieces, flat)
-    mine = added(exchange(spread(mine, line), line_axes), line)
-    gram = exchange(spread(mine, flat), plane_axes).reshape(depth, LANES)
+    gram = partial_gram.reshape(depth // SLAB, SLAB, LANES)
+    for axes in (core_axes, plane_axes):
+        gram = added(exchange(gram, axes), lax.axis_size(axes))
+    line = lax.axis_size(line_axes)
+    gram = added(exchange(spread(gram, line), line_axes), line)
+    for axes in (plane_axes, core_axes):
+        gram = exchange(spread(gram, lax.axis_size(axes)), axes)
+    gram = gram.reshape(depth, LANES)
 
     plane_core = pl.pallas_call(
         core_kernel,
@@ -177,7 +178,7 @@
     def program(field, start):
         count = field.shape[0] * field.shape[1] * field.shape[3]
         body = functools.partial(
-            shards, count, ("y", "core"), ("y", "core", "z_pair", "x"), ("z_mid", "z_hi")
+            shards, count, ("y", "core"), "core", ("y", "z_pair", "x"), ("z_mid", "z_hi")
         )
         return jax.shard_map(
             body, mesh=fine, in_specs=(placed, P()), out_specs=placed, check_vma=False

time: 119 us -> 119 us (level)
    all_to_all x5 -> x7, blocking collectives: 108 us -> 108 us  [exchange(): return lax.all_to_all(x, axes, 0, 0, tiled=True)]
where the time goes in v5:
time: 119 us
  blocking collectives  108 us (91%)
  Pallas kernels  9.66 us (8%)
    all_to_all x7, blocking collectives, exchange(): return lax.all_to_all(x, axes, 0, 0, tiled=True)  108 us
    pallas_call x1, Pallas kernels, shards(): pl.pallas_call(core_kernel, in_specs=[VMEM] * 3, out_specs=VMEM, out_shap...  8.23 us

profile of v5, /device:TPU:1, one launch (start us, length us, event | category | flops | bytes accessed | tf_op | source)
XLA Modules:
  0.0 118.5 jit_solution(8078255331368880695)
XLA Ops:
  0.0 36.9 %all_to_all.35 = f32[8,64,1024]{2,1,0:T(8,128)S(1)} all-to-all(f32[8,64,1024]{2,1,0:T(8,128)} %bitcast.21), channel_id=1, replica_groups=mesh['y'=4,'core'=2,'z_mid'=4,'z_pair'=2,'x'=4,'z_hi'=2] {'y','core'}, dimensions={0} | all-to-all | bytes 4194304 | tf_op jit(solution)/shard_map/all_to_all | solution.py:117
  36.9 1.4 %shard_map.28 = f32[1280,128]{1,0:T(8,128)S(1)} custom-call(f32[512,1024]{1,0:T(8,128)S(1)} %bitcast.13), custom_call_target="tpu_custom_call" | custom-call | tf_op jit(solution)/shard_map/pallas_call | solution.py:141
  38.3 4.9 %all_to_all.36 = f32[320,4,128]{2,1,0:T(4,128)S(1)} all-to-all(f32[320,4,128]{2,1,0:T(4,128)S(1)} %bitcast.16), channel_id=1, replica_groups=mesh['y'=4,'core'=2,'z_mid'=4,'z_pair'=2,'x'=4,'z_hi'=2] {'core'}, dimensions={0} | all-to-all | bytes 1310720 | tf_op jit(solution)/shard_map/all_to_all | solution.py:117
  43.2 0.2 reduce_sum.27
  43.5 11.5 %all_to_all.37 = f32[160,4,128]{2,1,0:T(4,128)S(1)} all-to-all(f32[160,4,128]{2,1,0:T(4,128)S(1)} %reduce_sum.27), channel_id=1, replica_groups=mesh['y'=4,'core'=2,'z_mid'=4,'z_pair'=2,'x'=4,'z_hi'=2] {'y','z_pair','x'}, dimensions={0} | all-to-all | bytes 655360 | tf_op jit(solution)/shard_map/all_to_all | solution.py:117
  55.0 0.0 copy-start
  55.0 0.1 reduce_sum.28
  55.1 23.6 %all_to_all.38 = f32[40,4,128]{2,1,0:T(4,128)S(1)} all-to-all(f32[40,4,128]{2,1,0:T(4,128)S(1)} %bitcast.26), channel_id=1, replica_groups=mesh['y'=4,'core'=2,'z_mid'=4,'z_pair'=2,'x'=4,'z_hi'=2] {'z_mid','z_hi'}, dimensions={0} | all-to-all | bytes 163840 | tf_op jit(solution)/shard_map/all_to_all | solution.py:117
  78.8 13.4 %all_to_all.39 = f32[160,4,128]{2,1,0:T(4,128)S(1)} all-to-all(f32[160,4,128]{2,1,0:T(4,128)S(1)} %bitcast.23), channel_id=1, replica_groups=mesh['y'=4,'core'=2,'z_mid'=4,'z_pair'=2,'x'=4,'z_hi'=2] {'y','z_pair','x'}, dimensions={0} | all-to-all | bytes 655360 | tf_op jit(solution)/shard_map/all_to_all | solution.py:117
  92.2 0.1 broadcast_in_dim.11
  92.3 8.0 %all_to_all.40 = f32[320,4,128]{2,1,0:T(4,128)S(1)} all-to-all(f32[320,4,128]{2,1,0:T(4,128)S(1)} %bitcast.20), channel_id=1, replica_groups=mesh['y'=4,'core'=2,'z_mid'=4,'z_pair'=2,'x'=4,'z_hi'=2] {'core'}, dimensions={0} | all-to-all | bytes 1310720 | tf_op jit(solution)/shard_map/all_to_all | solution.py:117
  100.2 0.0 copy-done
  100.2 8.2 %shard_map.29 = f32[64,1024]{1,0:T(8,128)S(1)} custom-call(f32[1280,128]{1,0:T(8,128)S(1)} %bitcast.15, f32[64,512]{1,0:T(8,128)S(1)} %bitcast.18, f32[512,1024]{1,0:T(8,128)S(1)} %bitcast.14), custom_call_target="tpu_custom_call" | custom-call | tf_op jit(solution)/shard_map/pallas_call | solution.py:158
  108.5 9.4 %all_to_all.41 = f32[8,8,1024]{2,1,0:T(8,128)S(1)} all-to-all(f32[8,8,1024]{2,1,0:T(8,128)S(1)} %bitcast.17), channel_id=1, replica_groups=mesh['y'=4,'core'=2,'z_mid'=4,'z_pair'=2,'x'=4,'z_hi'=2] {'y','core'}, dimensions={0} | all-to-all | bytes 524288 | tf_op jit(solution)/shard_map/all_to_all | solution.py:117
  117.8 0.7 copy.8
  (3 shorter events, 0.1 us)
Async XLA Ops:
  55.0 45.3 %copy-start = (f32[512,64]{0,1:T(8,128)S(1)}, f32[512,64]{0,1:T(8,128)}, u32[]{:S(2)}) copy-start(f32[512,64]{0,1:T(8,128)} %param.3) | copy-start | bytes 393220

commit v6 on v5

--- a/solution.py
+++ b/solution.py
@@ -41,7 +41,7 @@
         out_ref[place * LANES : (place + 1) * LANES, :] = part[r : r + LANES, c : c + LANES] * scale
 
 
-def inverse_factor(work):
+def inverse_factor(work, column_ref):
     n = work.shape[0]
     shape = (8, 2 * n)
     panels = n // 8
@@ -50,67 +50,62 @@
     done = []
     for p in range(panels):
         at = n + 8 * p
-        columns_of = [jnp.broadcast_to(tiles[p][:, at + j : at + j + 1], shape) for j in range(8)]
+        rest = range(p + 1, panels)
+
+        def column(tile, j):
+            return jnp.broadcast_to(tile[:, at + j : at + j + 1], shape)
+
+        for j in range(8):
+            column_ref[p, j] = column(tiles[p], j)
         rows = [jnp.broadcast_to(tiles[p][i : i + 1], shape) for i in range(8)]
         pivot = {
-            (i, j): jnp.broadcast_to(columns_of[j][i : i + 1], shape) for j in range(8) for i in range(j, 8)
+            (i, j): jnp.broadcast_to(column_ref[p, j, i : i + 1, :], shape)
+            for j in range(8)
+            for i in range(j, 8)
         }
-        factor, inverse = {}, []
+        below = {t: [column(tiles[t], j) for j in range(8)] for t in rest}
+        factor, scaled = {}, []
         for i in range(8):
-            inverse.append(1.0 / pivot[i, i])
+            inverse = 1.0 / pivot[i, i]
+            scaled.append(rows[i] * inverse)
             for j in range(i + 1, 8):
-                factor[j, i] = pivot[j, i] * inverse[i]
+                factor[j, i] = pivot[j, i] * inverse
             for j in range(i + 1, 8):
                 for m in range(i + 1, j + 1):
                     pivot[j, m] = pivot[j, m] - factor[j, i] * pivot[m, i]
                 rows[j] = rows[j] - factor[j, i] * rows[i]
+            for t in rest:
+                tiles[t] = tiles[t] - below[t][i] * scaled[i]
+                for j in range(i + 1, 8):
+                    below[t][j] = below[t][j] - factor[j, i] * below[t][i]
         final = rows[0] * lax.rsqrt(pivot[0, 0])
         for i in range(1, 8):
             final = jnp.where(sub == i, rows[i] * lax.rsqrt(pivot[i, i]), final)
         done.append(final)
-        solved = [None] * 8
-        for i in range(7, -1, -1):
-            value = rows[i] * inverse[i]
-            for k in range(i + 1, 8):
-                value = value - factor[k, i] * solved[k]
-            solved[i] = value
-        for t in range(p + 1, panels):
-            terms = [
-                jnp.broadcast_to(tiles[t][:, at + j : at + j + 1], shape) * solved[j] for j in range(8)
-            ]
-            while len(terms) > 1:
-                terms = [x + y for x, y in zip(terms[::2], terms[1::2])]
-            tiles[t] = tiles[t] - terms[0]
     return jnp.concatenate(done, axis=0)[:, :n]
 
 
-def core_kernel(gram_ref, start_ref, wide_ref, out_ref, full_ref):
+def core_kernel(gram_ref, start_ref, wide_ref, out_ref, full_ref, column_ref):
     order = full_ref.shape[0]
     for place, (i, j) in enumerate(blocks(order)):
         block = gram_ref[place * LANES : (place + 1) * LANES, :]
         full_ref[i * LANES : (i + 1) * LANES, j * LANES : (j + 1) * LANES] = block
         if i != j:
             full_ref[j * LANES : (j + 1) * LANES, i * LANES : (i + 1) * LANES] = block.T
-    dot = functools.partial(jnp.dot, precision=lax.Precision.HIGHEST, preferred_element_type=jnp.float32)
-    basis = start_ref[...]
-    rank = basis.shape[0]
+    dot = functools.partial(
+        lax.dot_general, precision=lax.Precision.HIGHEST, preferred_element_type=jnp.float32
+    )
+    plain, across = (((1,), (0,)), ((), ())), (((1,), (1,)), ((), ()))
+    rank = start_ref.shape[0]
     shape = (rank, 2 * rank)
     row, lane = (lax.broadcasted_iota(jnp.int32, shape, axis) for axis in (0, 1))
     eye = (row == lane).astype(jnp.float32)
+    image = dot(start_ref[...], full_ref[...], plain)
     for step in range(ITERS):
-        image = dot(basis, full_ref[...])
-        small = lax.dot_general(
-            image,
-            jnp.concatenate([jnp.zeros_like(image), image], axis=0),
-            (((1,), (1,)), ((), ())),
-            precision=lax.Precision.HIGHEST,
-            preferred_element_type=jnp.float32,
-        )
-        basis = dot(inverse_factor(small + eye), image)
-    high, low = split(basis)
-    part_high, part_low = split(wide_ref[...])
-    two = functools.partial(jnp.dot, preferred_element_type=jnp.float32)
-    out_ref[...] = two(high, part_high) + (two(high, part_low) + two(low, part_high))
+        small = dot(image, jnp.concatenate([jnp.zeros_like(image), image], axis=0), across)
+        follow = dot(image, full_ref[...] if step + 1 < ITERS else wide_ref[...], plain)
+        image = dot(inverse_factor(small + eye, column_ref), follow, plain)
+    out_ref[...] = image
 
 
 def exchange(x, axes):
@@ -160,7 +155,10 @@
         in_specs=[VMEM] * 3,
         out_specs=VMEM,
         out_shape=jax.ShapeDtypeStruct((rank, wide.shape[1]), jnp.float32),
-        scratch_shapes=[pltpu.VMEM((order, order), jnp.float32)],
+        scratch_shapes=[
+            pltpu.VMEM((order, order), jnp.float32),
+            pltpu.VMEM((rank // 8, 8, 8, 2 * rank), jnp.float32),
+        ],
         compiler_params=params,
     )(gram, start.T, wide)
     plane_core = plane_core.reshape(rank, moments // groups, planes)

time: 119 us -> 118 us (level)
  Pallas kernels: 9.66 us -> 8.26 us
    pallas_call x1, Pallas kernels: 8.23 us -> 6.83 us  [shards(): pl.pallas_call(core_kernel, in_specs=[VMEM] * 3, out_specs=VMEM, out_shap...]
where the time goes in v6:
time: 118 us; the launch traced here: 117 us
  blocking collectives  108 us (92%)
  Pallas kernels  8.26 us (7%)
    all_to_all x7, blocking collectives, exchange(): return lax.all_to_all(x, axes, 0, 0, tiled=True)  108 us
    pallas_call x1, Pallas kernels, shards(): pl.pallas_call(core_kernel, in_specs=[VMEM] * 3, out_specs=VMEM, out_shap...  6.83 us

profile of v6, /device:TPU:1, one launch (start us, length us, event | category | flops | bytes accessed | tf_op | source)
XLA Modules:
  0.0 117.2 jit_solution(2478274415017678277)
XLA Ops:
  0.0 36.9 %all_to_all.35 = f32[8,64,1024]{2,1,0:T(8,128)S(1)} all-to-all(f32[8,64,1024]{2,1,0:T(8,128)} %bitcast.21), channel_id=1, replica_groups=mesh['y'=4,'core'=2,'z_mid'=4,'z_pair'=2,'x'=4,'z_hi'=2] {'y','core'}, dimensions={0} | all-to-all | bytes 4194304 | tf_op jit(solution)/shard_map/all_to_all | solution.py:112
  36.9 1.4 %shard_map.28 = f32[1280,128]{1,0:T(8,128)S(1)} custom-call(f32[512,1024]{1,0:T(8,128)S(1)} %bitcast.13), custom_call_target="tpu_custom_call" | custom-call | tf_op jit(solution)/shard_map/pallas_call | solution.py:136
  38.3 4.9 %all_to_all.36 = f32[320,4,128]{2,1,0:T(4,128)S(1)} all-to-all(f32[320,4,128]{2,1,0:T(4,128)S(1)} %bitcast.16), channel_id=1, replica_groups=mesh['y'=4,'core'=2,'z_mid'=4,'z_pair'=2,'x'=4,'z_hi'=2] {'core'}, dimensions={0} | all-to-all | bytes 1310720 | tf_op jit(solution)/shard_map/all_to_all | solution.py:112
  43.2 0.2 reduce_sum.27
  43.5 11.5 %all_to_all.37 = f32[160,4,128]{2,1,0:T(4,128)S(1)} all-to-all(f32[160,4,128]{2,1,0:T(4,128)S(1)} %reduce_sum.27), channel_id=1, replica_groups=mesh['y'=4,'core'=2,'z_mid'=4,'z_pair'=2,'x'=4,'z_hi'=2] {'y','z_pair','x'}, dimensions={0} | all-to-all | bytes 655360 | tf_op jit(solution)/shard_map/all_to_all | solution.py:112
  55.0 0.0 copy-start
  55.0 0.1 reduce_sum.28
  55.1 23.6 %all_to_all.38 = f32[40,4,128]{2,1,0:T(4,128)S(1)} all-to-all(f32[40,4,128]{2,1,0:T(4,128)S(1)} %bitcast.26), channel_id=1, replica_groups=mesh['y'=4,'core'=2,'z_mid'=4,'z_pair'=2,'x'=4,'z_hi'=2] {'z_mid','z_hi'}, dimensions={0} | all-to-all | bytes 163840 | tf_op jit(solution)/shard_map/all_to_all | solution.py:112
  78.8 13.4 %all_to_all.39 = f32[160,4,128]{2,1,0:T(4,128)S(1)} all-to-all(f32[160,4,128]{2,1,0:T(4,128)S(1)} %bitcast.23), channel_id=1, replica_groups=mesh['y'=4,'core'=2,'z_mid'=4,'z_pair'=2,'x'=4,'z_hi'=2] {'y','z_pair','x'}, dimensions={0} | all-to-all | bytes 655360 | tf_op jit(solution)/shard_map/all_to_all | solution.py:112
  92.2 0.1 broadcast_in_dim.11
  92.3 8.0 %all_to_all.40 = f32[320,4,128]{2,1,0:T(4,128)S(1)} all-to-all(f32[320,4,128]{2,1,0:T(4,128)S(1)} %bitcast.20), channel_id=1, replica_groups=mesh['y'=4,'core'=2,'z_mid'=4,'z_pair'=2,'x'=4,'z_hi'=2] {'core'}, dimensions={0} | all-to-all | bytes 1310720 | tf_op jit(solution)/shard_map/all_to_all | solution.py:112
  100.2 0.0 copy-done
  100.2 6.8 %shard_map.29 = f32[64,1024]{1,0:T(8,128)S(1)} custom-call(f32[1280,128]{1,0:T(8,128)S(1)} %bitcast.15, f32[64,512]{1,0:T(8,128)S(1)} %bitcast.18, f32[512,1024]{1,0:T(8,128)S(1)} %bitcast.14), custom_call_target="tpu_custom_call" | custom-call | tf_op jit(solution)/shard_map/pallas_call | solution.py:153
  107.1 9.4 %all_to_all.41 = f32[8,8,1024]{2,1,0:T(8,128)S(1)} all-to-all(f32[8,8,1024]{2,1,0:T(8,128)S(1)} %bitcast.17), channel_id=1, replica_groups=mesh['y'=4,'core'=2,'z_mid'=4,'z_pair'=2,'x'=4,'z_hi'=2] {'y','core'}, dimensions={0} | all-to-all | bytes 524288 | tf_op jit(solution)/shard_map/all_to_all | solution.py:112
  116.5 0.7 copy.8
  (3 shorter events, 0.1 us)
Async XLA Ops:
  55.0 45.3 %copy-start = (f32[512,64]{0,1:T(8,128)S(1)}, f32[512,64]{0,1:T(8,128)}, u32[]{:S(2)}) copy-start(f32[512,64]{0,1:T(8,128)} %param.3) | copy-start | bytes 393220

commit v7 on v6

--- a/solution.py
+++ b/solution.py
@@ -9,7 +9,9 @@
 
 ITERS = 2
 LANES = 128
-SLAB = 4
+HALF = LANES // 2
+SLAB = 2
+CHUNK = 16
 VMEM = pl.BlockSpec(memory_space=pltpu.VMEM)
 
 
@@ -20,10 +22,14 @@
 
 def blocks(order):
     count = order // LANES
-    return [(i, j) for i in range(count) for j in range(i, count)]
-
-
-def gram_kernel(scale, wide_ref, out_ref):
+    return [(i, j) for i in range(count) for j in range(i + 1, count)]
+
+
+def depth_of(order):
+    return len(blocks(order)) * LANES + order // LANES * HALF * 3 // 2
+
+
+def gram_kernel(scale, cores, chips, wide_ref, out_ref):
     high, low = split(wide_ref[...])
     order = high.shape[0]
     half = order // 2
@@ -35,10 +41,47 @@
             a, b = slice(i * half, (i + 1) * half), slice(j * half, (j + 1) * half)
             parts[i, j] = dot(high[a], high[b]) + (dot(high[a], low[b]) + dot(low[a], high[b]))
     per = half // LANES
-    for place, (i, j) in enumerate(blocks(order)):
-        part = parts[i // per, j // per]
+    share = out_ref.shape[0] // (cores * chips)
+    row = 0
+
+    def block(i, j):
         r, c = (i % per) * LANES, (j % per) * LANES
-        out_ref[place * LANES : (place + 1) * LANES, :] = part[r : r + LANES, c : c + LANES] * scale
+        return parts[i // per, j // per][r : r + LANES, c : c + LANES] * scale
+
+    def store(row, value):
+        for at in range(0, value.shape[0], CHUNK):
+            group, inside = divmod(row + at, share)
+            core, chip = divmod(group, chips)
+            to = (chip * cores + core) * share + inside
+            out_ref[to : to + CHUNK, :] = value[at : at + CHUNK]
+        return row + value.shape[0]
+
+    for i, j in blocks(order):
+        row = store(row, block(i, j))
+    for i in range(0, order // LANES, 2):
+        first, second = block(i, i), block(i + 1, i + 1)
+        row = store(row, first[:HALF])
+        row = store(row, second[:HALF])
+        row = store(row, jnp.concatenate([first[HALF:, HALF:], second[HALF:, HALF:]], axis=1))
+
+
+def unpack(gram_ref, full_ref):
+    order = full_ref.shape[0]
+    row = 0
+    for i, j in blocks(order):
+        part = gram_ref[row : row + LANES, :]
+        full_ref[i * LANES : (i + 1) * LANES, j * LANES : (j + 1) * LANES] = part
+        full_ref[j * LANES : (j + 1) * LANES, i * LANES : (i + 1) * LANES] = part.T
+        row += LANES
+    for i in range(0, order // LANES, 2):
+        ends = gram_ref[row + LANES : row + LANES + HALF, :]
+        for k in range(2):
+            at = (i + k) * LANES
+            top = gram_ref[row + k * HALF : row + (k + 1) * HALF, :]
+            bottom = [top[:, HALF:].T, ends[:, k * HALF : (k + 1) * HALF]]
+            full_ref[at : at + HALF, at : at + LANES] = top
+            full_ref[at + HALF : at + LANES, at : at + LANES] = jnp.concatenate(bottom, axis=1)
+        row += LANES + HALF
 
 
 def inverse_factor(work, column_ref):
@@ -86,12 +129,7 @@
 
 
 def core_kernel(gram_ref, start_ref, wide_ref, out_ref, full_ref, column_ref):
-    order = full_ref.shape[0]
-    for place, (i, j) in enumerate(blocks(order)):
-        block = gram_ref[place * LANES : (place + 1) * LANES, :]
-        full_ref[i * LANES : (i + 1) * LANES, j * LANES : (j + 1) * LANES] = block
-        if i != j:
-            full_ref[j * LANES : (j + 1) * LANES, i * LANES : (i + 1) * LANES] = block.T
+    unpack(gram_ref, full_ref)
     dot = functools.partial(
         lax.dot_general, precision=lax.Precision.HIGHEST, preferred_element_type=jnp.float32
     )
@@ -121,7 +159,7 @@
     return copies.reshape(count * block.shape[0], *block.shape[1:])
 
 
-def shards(count, group_axes, core_axes, plane_axes, line_axes, field, start):
+def shards(count, group_axes, all_axes, core_axes, plane_axes, line_axes, field, start):
     groups = lax.axis_size(group_axes)
     times, species, rows, planes = field.shape
     moments = times * species
@@ -132,9 +170,10 @@
     wide = wide.reshape(groups, moments // groups, rows, planes)
     wide = jnp.moveaxis(wide, 1, 2).reshape(order, moments // groups * planes)
 
-    depth = len(blocks(order)) * LANES
+    depth = depth_of(order)
+    cores = lax.axis_size(core_axes)
     partial_gram = pl.pallas_call(
-        functools.partial(gram_kernel, 1.0 / count),
+        functools.partial(gram_kernel, 1.0 / count, cores, groups // cores),
         in_specs=[VMEM],
         out_specs=VMEM,
         out_shape=jax.ShapeDtypeStruct((depth, LANES), jnp.float32),
@@ -142,8 +181,7 @@
     )(wide)
 
     gram = partial_gram.reshape(depth // SLAB, SLAB, LANES)
-    for axes in (core_axes, plane_axes):
-        gram = added(exchange(gram, axes), lax.axis_size(axes))
+    gram = added(exchange(gram, all_axes), lax.axis_size(all_axes))
     line = lax.axis_size(line_axes)
     gram = added(exchange(spread(gram, line), line_axes), line)
     for axes in (plane_axes, core_axes):
@@ -176,7 +214,13 @@
     def program(field, start):
         count = field.shape[0] * field.shape[1] * field.shape[3]
         body = functools.partial(
-            shards, count, ("y", "core"), "core", ("y", "z_pair", "x"), ("z_mid", "z_hi")
+            shards,
+            count,
+            ("y", "core"),
+            ("y", "core", "z_pair", "x"),
+            "core",
+            ("y", "z_pair", "x"),
+            ("z_mid", "z_hi"),
         )
         return jax.shard_map(
             body, mesh=fine, in_specs=(placed, P()), out_specs=placed, check_vma=False

time: 118 us -> 117 us (level)
    all_to_all x7 -> x6, blocking collectives: 108 us -> 107 us  [exchange(): return lax.all_to_all(x, axes, 0, 0, tiled=True)]
where the time goes in v7:
time: 117 us; the launch traced here: 116 us
  blocking collectives  107 us (91%)
  Pallas kernels  8.29 us (7%)
    all_to_all x6, blocking collectives, exchange(): return lax.all_to_all(x, axes, 0, 0, tiled=True)  107 us
    pallas_call x1, Pallas kernels, shards(): pl.pallas_call(core_kernel, in_specs=[VMEM] * 3, out_specs=VMEM, out_shap...  6.83 us

profile of v7, /device:TPU:1, one launch (start us, length us, event | category | flops | bytes accessed | tf_op | source)
XLA Modules:
  0.0 116.2 jit_solution(2863876699679485286)
XLA Ops:
  0.0 36.9 %all_to_all.30 = f32[8,64,1024]{2,1,0:T(8,128)S(1)} all-to-all(f32[8,64,1024]{2,1,0:T(8,128)} %bitcast.20), channel_id=1, replica_groups=mesh['y'=4,'core'=2,'z_mid'=4,'z_pair'=2,'x'=4,'z_hi'=2] {'y','core'}, dimensions={0} | all-to-all | bytes 4194304 | tf_op jit(solution)/shard_map/all_to_all | solution.py:150
  36.9 1.5 %shard_map.28 = f32[1152,128]{1,0:T(8,128)S(1)} custom-call(f32[512,1024]{1,0:T(8,128)S(1)} %bitcast.12), custom_call_target="tpu_custom_call" | custom-call | tf_op jit(solution)/shard_map/pallas_call | solution.py:175
  38.3 17.5 %all_to_all.31 = f32[576,2,128]{2,1,0:T(2,128)S(1)} all-to-all(f32[576,2,128]{2,1,0:T(2,128)S(1)} %bitcast.15), channel_id=1, replica_groups=mesh['y'=4,'core'=2,'z_mid'=4,'z_pair'=2,'x'=4,'z_hi'=2] {'y','core','z_..., dimensions={0} | all-to-all | bytes 1179648 | tf_op jit(solution)/shard_map/all_to_all | solution.py:150
  55.8 0.0 copy-start
  55.8 0.2 reduce_sum.18
  56.1 23.9 %all_to_all.32 = f32[72,2,128]{2,1,0:T(2,128)S(1)} all-to-all(f32[72,2,128]{2,1,0:T(2,128)S(1)} %bitcast.24), channel_id=1, replica_groups=mesh['y'=4,'core'=2,'z_mid'=4,'z_pair'=2,'x'=4,'z_hi'=2] {'z_mid','z_hi'}, dimensions={0} | all-to-all | bytes 147456 | tf_op jit(solution)/shard_map/all_to_all | solution.py:150
  80.0 0.1 broadcast_in_dim.10
  80.1 11.3 %all_to_all.33 = f32[288,2,128]{2,1,0:T(2,128)S(1)} all-to-all(f32[288,2,128]{2,1,0:T(2,128)S(1)} %bitcast.21), channel_id=1, replica_groups=mesh['y'=4,'core'=2,'z_mid'=4,'z_pair'=2,'x'=4,'z_hi'=2] {'y','z_pair','x'}, dimensions={0} | all-to-all | bytes 589824 | tf_op jit(solution)/shard_map/all_to_all | solution.py:150
  91.5 0.2 broadcast_in_dim.11
  91.6 7.7 %all_to_all.34 = f32[576,2,128]{2,1,0:T(2,128)S(1)} all-to-all(f32[576,2,128]{2,1,0:T(2,128)S(1)} %bitcast.19), channel_id=1, replica_groups=mesh['y'=4,'core'=2,'z_mid'=4,'z_pair'=2,'x'=4,'z_hi'=2] {'core'}, dimensions={0} | all-to-all | bytes 1179648 | tf_op jit(solution)/shard_map/all_to_all | solution.py:150
  99.3 0.0 copy-done
  99.3 6.8 %shard_map.29 = f32[64,1024]{1,0:T(8,128)S(1)} custom-call(f32[1152,128]{1,0:T(8,128)S(1)} %bitcast.14, f32[64,512]{1,0:T(8,128)S(1)} %bitcast.17, f32[512,1024]{1,0:T(8,128)S(1)} %bitcast.13), custom_call_target="tpu_custom_call" | custom-call | tf_op jit(solution)/shard_map/pallas_call | solution.py:191
  106.2 9.4 %all_to_all.35 = f32[8,8,1024]{2,1,0:T(8,128)S(1)} all-to-all(f32[8,8,1024]{2,1,0:T(8,128)S(1)} %bitcast.16), channel_id=1, replica_groups=mesh['y'=4,'core'=2,'z_mid'=4,'z_pair'=2,'x'=4,'z_hi'=2] {'y','core'}, dimensions={0} | all-to-all | bytes 524288 | tf_op jit(solution)/shard_map/all_to_all | solution.py:150
  115.5 0.7 copy.6
  (2 shorter events, 0.1 us)
Async XLA Ops:
  55.8 43.5 %copy-start = (f32[512,64]{0,1:T(8,128)S(1)}, f32[512,64]{0,1:T(8,128)}, u32[]{:S(2)}) copy-start(f32[512,64]{0,1:T(8,128)} %param.3) | copy-start | bytes 393220

commit v8 on v7

--- a/solution.py
+++ b/solution.py
@@ -128,7 +128,10 @@
     return jnp.concatenate(done, axis=0)[:, :n]
 
 
-def core_kernel(gram_ref, start_ref, wide_ref, out_ref, full_ref, column_ref):
+def core_kernel(place_ref, mine_ref, other_ref, start_ref, wide_ref, out_ref, gram_ref, full_ref, column_ref):
+    size = mine_ref.shape[0]
+    for part_ref, place in ((mine_ref, place_ref[0]), (other_ref, 1 - place_ref[0])):
+        gram_ref[pl.ds(pl.multiple_of(place * size, 8), size), :] = part_ref[...]
     unpack(gram_ref, full_ref)
     dot = functools.partial(
         lax.dot_general, precision=lax.Precision.HIGHEST, preferred_element_type=jnp.float32
@@ -184,21 +187,23 @@
     gram = added(exchange(gram, all_axes), lax.axis_size(all_axes))
     line = lax.axis_size(line_axes)
     gram = added(exchange(spread(gram, line), line_axes), line)
-    for axes in (plane_axes, core_axes):
-        gram = exchange(spread(gram, lax.axis_size(axes)), axes)
-    gram = gram.reshape(depth, LANES)
+    mine = exchange(spread(gram, lax.axis_size(plane_axes)), plane_axes)
+    mine = mine.reshape(depth // cores, LANES)
+    other = lax.ppermute(mine, core_axes, [(0, 1), (1, 0)])
+    place = lax.axis_index(core_axes).astype(jnp.int32).reshape(1)
 
     plane_core = pl.pallas_call(
         core_kernel,
-        in_specs=[VMEM] * 3,
+        in_specs=[pl.BlockSpec(memory_space=pltpu.SMEM)] + [VMEM] * 4,
         out_specs=VMEM,
         out_shape=jax.ShapeDtypeStruct((rank, wide.shape[1]), jnp.float32),
         scratch_shapes=[
+            pltpu.VMEM((depth, LANES), jnp.float32),
             pltpu.VMEM((order, order), jnp.float32),
             pltpu.VMEM((rank // 8, 8, 8, 2 * rank), jnp.float32),
         ],
         compiler_params=params,
-    )(gram, start.T, wide)
+    )(place, mine, other, start.T, wide)
     plane_core = plane_core.reshape(rank, moments // groups, planes)
     plane_core = plane_core.reshape(groups, rank // groups, moments // groups, planes)
     core = exchange(jnp.moveaxis(plane_core, 2, 1).reshape(moments, rank // groups, planes), group_axes)

time: 117 us -> 116 us (level)
  blocking collectives: 107 us -> 99.1 us
  starting transfers between devices: 0 us -> 5.79 us
  waiting for transfers between devices: 0 us -> 1.18 us
    all_to_all x6 -> x5, blocking collectives: 107 us -> 99.1 us  [exchange(): return lax.all_to_all(x, axes, 0, 0, tiled=True)]
    ppermute x0 -> x1, starting transfers between devices: none -> 5.79 us  [shards(): other = lax.ppermute(mine, core_axes, [(0, 1), (1, 0)])]
    ppermute x0 -> x1, waiting for transfers between devices: none -> 1.18 us  [shards(): other = lax.ppermute(mine, core_axes, [(0, 1), (1, 0)])]
  transfers between devices with their start and end apart: 0 -> 1, of which waited for: 0 -> 1; matrix products, arithmetic and copies ran while one was open for 0% -> 0% of each run, Pallas kernels for 0% -> 0%
where the time goes in v8:
time: 116 us
  blocking collectives  99.1 us (85%)
  Pallas kernels  8.33 us (7%)
  starting transfers between devices  5.79 us (5%)
  waiting for transfers between devices  1.18 us (1%)
    all_to_all x5, blocking collectives, exchange(): return lax.all_to_all(x, axes, 0, 0, tiled=True)  99.1 us
    pallas_call x1, Pallas kernels, shards(): pl.pallas_call(core_kernel, in_specs=[pl.BlockSpec(memory_space=pltpu.SME...  6.86 us
    ppermute x1, starting transfers between devices, shards(): other = lax.ppermute(mine, core_axes, [(0, 1), (1, 0)])  5.79 us
  transfers between devices with their start and end apart: 1, of which 1 were waited for; matrix products, arithmetic and copies ran while one was open for 0% of the time, Pallas kernels for 0%

profile of v8, /device:TPU:1, one launch (start us, length us, event | category | flops | bytes accessed | tf_op | source)
XLA Modules:
  0.0 115.5 jit_solution(3026081234243306729)
XLA Ops:
  0.0 36.9 %all_to_all.25 = f32[8,64,1024]{2,1,0:T(8,128)S(1)} all-to-all(f32[8,64,1024]{2,1,0:T(8,128)} %bitcast.20), channel_id=1, replica_groups=mesh['y'=4,'core'=2,'z_mid'=4,'z_pair'=2,'x'=4,'z_hi'=2] {'y','core'}, dimensions={0} | all-to-all | bytes 4194304 | tf_op jit(solution)/shard_map/all_to_all | solution.py:153
  36.9 1.5 %shard_map.28 = f32[1152,128]{1,0:T(8,128)S(1)} custom-call(f32[512,1024]{1,0:T(8,128)S(1)} %bitcast.12), custom_call_target="tpu_custom_call" | custom-call | tf_op jit(solution)/shard_map/pallas_call | solution.py:178
  38.3 0.0 copy-start
  38.3 17.6 %all_to_all.26 = f32[576,2,128]{2,1,0:T(2,128)S(1)} all-to-all(f32[576,2,128]{2,1,0:T(2,128)S(1)} %bitcast.14), channel_id=1, replica_groups=mesh['y'=4,'core'=2,'z_mid'=4,'z_pair'=2,'x'=4,'z_hi'=2] {'y','core','z_..., dimensions={0} | all-to-all | bytes 1179648 | tf_op jit(solution)/shard_map/all_to_all | solution.py:153
  56.0 0.2 reduce_sum.18
  56.2 23.9 %all_to_all.27 = f32[72,2,128]{2,1,0:T(2,128)S(1)} all-to-all(f32[72,2,128]{2,1,0:T(2,128)S(1)} %bitcast.24), channel_id=1, replica_groups=mesh['y'=4,'core'=2,'z_mid'=4,'z_pair'=2,'x'=4,'z_hi'=2] {'z_mid','z_hi'}, dimensions={0} | all-to-all | bytes 147456 | tf_op jit(solution)/shard_map/all_to_all | solution.py:153
  80.2 0.1 broadcast_in_dim.7
  80.3 11.3 %all_to_all.28 = f32[288,2,128]{2,1,0:T(2,128)S(1)} all-to-all(f32[288,2,128]{2,1,0:T(2,128)S(1)} %bitcast.21), channel_id=1, replica_groups=mesh['y'=4,'core'=2,'z_mid'=4,'z_pair'=2,'x'=4,'z_hi'=2] {'y','z_pair','x'}, dimensions={0} | all-to-all | bytes 589824 | tf_op jit(solution)/shard_map/all_to_all | solution.py:153
  91.6 5.8 %collective-permute-start = (f32[576,128]{1,0:T(8,128)S(1)}, f32[576,128]{1,0:T(8,128)S(1)}, u32[]{:S(2)}, u32[]{:S(2)}) collective-permute-start(f32[576,128]{1,0:T(8,128)S(1)} %bitcast.15), channel_id=1, source_target_pairs={{0,64},{64,0},{1,65},{65,1},{2,66},{66,2},{3,67},{67,3},{4,68},{68... | collective-permute-start | bytes 884744 | tf_op jit(solution)/shard_map/ppermute | solution.py:192
  97.4 1.2 %collective-permute-done.other_ref = f32[576,128]{1,0:T(8,128)S(1)} collective-permute-done((f32[576,128]{1,0:T(8,128)S(1)}, f32[576,128]{1,0:T(8,128)S(1)}, u32[]{:S(2)}, u32[]{:S(2)}) %collective-permute-start) | collective-permute-done | bytes 294944 | tf_op jit(solution)/shard_map/ppermute | solution.py:192
  98.6 0.0 copy-done
  98.6 6.9 %shard_map.29 = f32[64,1024]{1,0:T(8,128)S(1)} custom-call(s32[1]{0:T(128)} %bitcast.place_ref, f32[576,128]{1,0:T(8,128)S(1)} %bitcast.16, f32[576,128]{1,0:T(8,128)S(1)} %collective-permute-done.other_ref, f32[64,512]{1,0:T(8,128)S(1)} %bitcast.18, f32[512,1024]{1,0:T(8,128)S(1)} %bitcast.13), custom_call_target="tpu_custom_call" | custom-call | tf_op jit(solution)/shard_map/pallas_call | solution.py:195
  105.5 9.4 %all_to_all.29 = f32[8,8,1024]{2,1,0:T(8,128)S(1)} all-to-all(f32[8,8,1024]{2,1,0:T(8,128)S(1)} %bitcast.17), channel_id=1, replica_groups=mesh['y'=4,'core'=2,'z_mid'=4,'z_pair'=2,'x'=4,'z_hi'=2] {'y','core'}, dimensions={0} | all-to-all | bytes 524288 | tf_op jit(solution)/shard_map/all_to_all | solution.py:153
  114.8 0.7 copy.6
  (2 shorter events, 0.1 us)
Async XLA Ops:
  38.3 60.3 %copy-start = (f32[512,64]{0,1:T(8,128)S(1)}, f32[512,64]{0,1:T(8,128)}, u32[]{:S(2)}) copy-start(f32[512,64]{0,1:T(8,128)} %param.3) | copy-start | bytes 393220
  91.6 7.0 %collective-permute-start = (f32[576,128]{1,0:T(8,128)S(1)}, f32[576,128]{1,0:T(8,128)S(1)}, u32[]{:S(2)}, u32[]{:S(2)}) collective-permute-start(f32[576,128]{1,0:T(8,128)S(1)} %bitcast.15), channel_id=1, source_target_pairs={{0,64},{64,0},{1,65},{65,1},{2,66},{66,2},{3,67},{67,3},{4,68},{68... | collective-permute-start | bytes 884744 | tf_op jit(solution)/shard_map/ppermute | solution.py:192

commit v9 on v8

--- a/solution.py
+++ b/solution.py
@@ -11,7 +11,6 @@
 LANES = 128
 HALF = LANES // 2
 SLAB = 2
-CHUNK = 16
 VMEM = pl.BlockSpec(memory_space=pltpu.VMEM)
 
 
@@ -29,7 +28,7 @@
     return len(blocks(order)) * LANES + order // LANES * HALF * 3 // 2
 
 
-def gram_kernel(scale, cores, chips, wide_ref, out_ref):
+def gram_kernel(scale, place_ref, wide_ref, keep_ref, send_ref, packed_ref):
     high, low = split(wide_ref[...])
     order = high.shape[0]
     half = order // 2
@@ -41,7 +40,6 @@
             a, b = slice(i * half, (i + 1) * half), slice(j * half, (j + 1) * half)
             parts[i, j] = dot(high[a], high[b]) + (dot(high[a], low[b]) + dot(low[a], high[b]))
     per = half // LANES
-    share = out_ref.shape[0] // (cores * chips)
     row = 0
 
     def block(i, j):
@@ -49,11 +47,7 @@
         return parts[i // per, j // per][r : r + LANES, c : c + LANES] * scale
 
     def store(row, value):
-        for at in range(0, value.shape[0], CHUNK):
-            group, inside = divmod(row + at, share)
-            core, chip = divmod(group, chips)
-            to = (chip * cores + core) * share + inside
-            out_ref[to : to + CHUNK, :] = value[at : at + CHUNK]
+        packed_ref[row : row + value.shape[0], :] = value
         return row + value.shape[0]
 
     for i, j in blocks(order):
@@ -63,6 +57,9 @@
         row = store(row, first[:HALF])
         row = store(row, second[:HALF])
         row = store(row, jnp.concatenate([first[HALF:, HALF:], second[HALF:, HALF:]], axis=1))
+    size = keep_ref.shape[0]
+    for part_ref, place in ((keep_ref, place_ref[0]), (send_ref, 1 - place_ref[0])):
+        part_ref[...] = packed_ref[pl.ds(pl.multiple_of(place * size, 8), size), :]
 
 
 def unpack(gram_ref, full_ref):
@@ -162,7 +159,7 @@
     return copies.reshape(count * block.shape[0], *block.shape[1:])
 
 
-def shards(count, group_axes, all_axes, core_axes, plane_axes, line_axes, field, start):
+def shards(count, group_axes, core_axes, plane_axes, line_axes, field, start):
     groups = lax.axis_size(group_axes)
     times, species, rows, planes = field.shape
     moments = times * species
@@ -175,26 +172,30 @@
 
     depth = depth_of(order)
     cores = lax.axis_size(core_axes)
-    partial_gram = pl.pallas_call(
-        functools.partial(gram_kernel, 1.0 / count, cores, groups // cores),
-        in_specs=[VMEM],
-        out_specs=VMEM,
-        out_shape=jax.ShapeDtypeStruct((depth, LANES), jnp.float32),
+    half = jax.ShapeDtypeStruct((depth // cores, LANES), jnp.float32)
+    place = lax.axis_index(core_axes).astype(jnp.int32).reshape(1)
+    scalar = pl.BlockSpec(memory_space=pltpu.SMEM)
+    keep, send = pl.pallas_call(
+        functools.partial(gram_kernel, 1.0 / count),
+        in_specs=[scalar, VMEM],
+        out_specs=[VMEM] * 2,
+        out_shape=[half] * 2,
+        scratch_shapes=[pltpu.VMEM((depth, LANES), jnp.float32)],
         compiler_params=params,
-    )(wide)
-
-    gram = partial_gram.reshape(depth // SLAB, SLAB, LANES)
-    gram = added(exchange(gram, all_axes), lax.axis_size(all_axes))
+    )(place, wide)
+
+    swap = functools.partial(lax.ppermute, axis_name=core_axes, perm=[(0, 1), (1, 0)])
+    gram = (keep + swap(send)).reshape(depth // cores // SLAB, SLAB, LANES)
+    gram = added(exchange(gram, plane_axes), lax.axis_size(plane_axes))
     line = lax.axis_size(line_axes)
     gram = added(exchange(spread(gram, line), line_axes), line)
     mine = exchange(spread(gram, lax.axis_size(plane_axes)), plane_axes)
     mine = mine.reshape(depth // cores, LANES)
-    other = lax.ppermute(mine, core_axes, [(0, 1), (1, 0)])
-    place = lax.axis_index(core_axes).astype(jnp.int32).reshape(1)
+    other = swap(mine)
 
     plane_core = pl.pallas_call(
         core_kernel,
-        in_specs=[pl.BlockSpec(memory_space=pltpu.SMEM)] + [VMEM] * 4,
+        in_specs=[scalar] + [VMEM] * 4,
         out_specs=VMEM,
         out_shape=jax.ShapeDtypeStruct((rank, wide.shape[1]), jnp.float32),
         scratch_shapes=[
@@ -222,7 +223,6 @@
             shards,
             count,
             ("y", "core"),
-            ("y", "core", "z_pair", "x"),
             "core",
             ("y", "z_pair", "x"),
             ("z_mid", "z_hi"),

time: 116 us -> 115 us (level)
  blocking collectives: 99.1 us -> 57.3 us
  waiting for transfers between devices: 1.18 us -> 28.7 us
  starting transfers between devices: 5.79 us -> 19.3 us
    all_to_all x5 -> x4, blocking collectives: 99.1 us -> 57.3 us  [exchange(): return lax.all_to_all(x, axes, 0, 0, tiled=True)]
    all_to_all x0 -> x1, waiting for transfers between devices: none -> 26.4 us  [exchange(): return lax.all_to_all(x, axes, 0, 0, tiled=True)]
    all_to_all x0 -> x1, starting transfers between devices: none -> 10.4 us  [exchange(): return lax.all_to_all(x, axes, 0, 0, tiled=True)]
    ppermute x1 -> x2, starting transfers between devices: 5.79 us -> 8.91 us  [the longest x1 6.13 us: shards(): other = swap(mine)]
    ppermute x1 -> x2, waiting for transfers between devices: 1.18 us -> 2.37 us  [the longest x1 1.19 us: shards(): gram = (keep + swap(send)).reshape(depth // cores // SLAB, SLAB, LANES)]
  transfers between devices with their start and end apart: 1 -> 3, of which waited for: 1 -> 3; matrix products, arithmetic and copies ran while one was open for 0% -> 0% of each run, Pallas kernels for 0% -> 0%
where the time goes in v9:
time: 115 us
  blocking collectives  57.3 us (50%)
  waiting for transfers between devices  28.7 us (25%)
  starting transfers between devices  19.3 us (17%)
  Pallas kernels  8.37 us (7%)
    all_to_all x4, blocking collectives, exchange(): return lax.all_to_all(x, axes, 0, 0, tiled=True)  57.3 us
    all_to_all x1, waiting for transfers between devices, exchange(): return lax.all_to_all(x, axes, 0, 0, tiled=True)  26.4 us
    all_to_all x1, starting transfers between devices, exchange(): return lax.all_to_all(x, axes, 0, 0, tiled=True)  10.4 us
    pallas_call x1, Pallas kernels, shards(): pl.pallas_call(core_kernel, in_specs=[scalar] + [VMEM] * 4, out_specs=VME...  6.86 us
    ppermute x1, starting transfers between devices, shards(): other = swap(mine)  6.13 us
    ppermute x1, starting transfers between devices, shards(): gram = (keep + swap(send)).reshape(depth // cores // SLAB, SLAB, LANES)  2.78 us
  transfers between devices with their start and end apart: 3, of which 3 were waited for; matrix products, arithmetic and copies ran while one was open for 0% of the time, Pallas kernels for 0%

profile of v9, /device:TPU:1, one launch (start us, length us, event | category | flops | bytes accessed | tf_op | source)
XLA Modules:
  0.0 114.7 jit_solution(9596318579181100758)
XLA Ops:
  0.0 10.4 %all-to-all-start = ((f32[8,64,1024]{2,1,0:T(8,128)}), f32[8,64,1024]{2,1,0:T(8,128)S(1)}, u32[]{:S(2)}, u32[]{:S(2)}) async-start(f32[8,64,1024]{2,1,0:T(8,128)} %bitcast.18), calls=%async_computation | async-start | bytes 4194304 | tf_op jit(solution)/shard_map/all_to_all | solution.py:150
  10.4 26.4 %all-to-all-done = f32[8,64,1024]{2,1,0:T(8,128)S(1)} async-done(((f32[8,64,1024]{2,1,0:T(8,128)}), f32[8,64,1024]{2,1,0:T(8,128)S(1)}, u32[]{:S(2)}, u32[]{:S(2)}) %all-to-all-start) | async-done | bytes 2097184 | tf_op jit(solution)/shard_map/all_to_all | solution.py:150
  36.7 0.0 copy-start
  36.7 1.5 %shard_map.28 = (f32[576,128]{1,0:T(8,128)S(1)}, f32[576,128]{1,0:T(8,128)S(1)}) custom-call(s32[1]{0:T(128)} %bitcast.place_ref, f32[512,1024]{1,0:T(8,128)S(1)} %bitcast.12), custom_call_target="tpu_custom_call" | custom-call | tf_op jit(solution)/shard_map/pallas_call | solution.py:178
  38.3 2.8 %collective-permute-start = (f32[576,128]{1,0:T(8,128)S(1)}, f32[576,128]{1,0:T(8,128)S(1)}, u32[]{:S(2)}, u32[]{:S(2)}) collective-permute-start(f32[576,128]{1,0:T(8,128)S(1)} %get-tuple-element.8), channel_id=1, source_target_pairs={{0,64},{64,0},{1,65},{65,1},{2,66},{66,2},{3,67},{67,3},{4,68},{68... | collective-permute-start | bytes 884744 | tf_op jit(solution)/shard_map/ppermute | solution.py:188
  41.0 1.2 %collective-permute-done = f32[576,128]{1,0:T(8,128)S(1)} collective-permute-done((f32[576,128]{1,0:T(8,128)S(1)}, f32[576,128]{1,0:T(8,128)S(1)}, u32[]{:S(2)}, u32[]{:S(2)}) %collective-permute-start) | collective-permute-done | bytes 294944 | tf_op jit(solution)/shard_map/ppermute | solution.py:188
  42.3 11.3 %all_to_all.25 = f32[288,2,128]{2,1,0:T(2,128)S(1)} all-to-all(f32[288,2,128]{2,1,0:T(2,128)S(1)} %bitcast.19), channel_id=1, replica_groups=mesh['y'=4,'core'=2,'z_mid'=4,'z_pair'=2,'x'=4,'z_hi'=2] {'y','z_pair','x'}, dimensions={0} | all-to-all | bytes 589824 | tf_op jit(solution)/shard_map/all_to_all | solution.py:150
  53.5 0.1 reduce_sum.18
  53.7 23.7 %all_to_all.26 = f32[72,2,128]{2,1,0:T(2,128)S(1)} all-to-all(f32[72,2,128]{2,1,0:T(2,128)S(1)} %bitcast.24), channel_id=1, replica_groups=mesh['y'=4,'core'=2,'z_mid'=4,'z_pair'=2,'x'=4,'z_hi'=2] {'z_mid','z_hi'}, dimensions={0} | all-to-all | bytes 147456 | tf_op jit(solution)/shard_map/all_to_all | solution.py:150
  77.4 0.1 broadcast_in_dim.7
  77.5 12.9 %all_to_all.27 = f32[288,2,128]{2,1,0:T(2,128)S(1)} all-to-all(f32[288,2,128]{2,1,0:T(2,128)S(1)} %bitcast.21), channel_id=1, replica_groups=mesh['y'=4,'core'=2,'z_mid'=4,'z_pair'=2,'x'=4,'z_hi'=2] {'y','z_pair','x'}, dimensions={0} | all-to-all | bytes 589824 | tf_op jit(solution)/shard_map/all_to_all | solution.py:150
  90.4 6.1 %collective-permute-start.1 = (f32[576,128]{1,0:T(8,128)S(1)}, f32[576,128]{1,0:T(8,128)S(1)}, u32[]{:S(2)}, u32[]{:S(2)}) collective-permute-start(f32[576,128]{1,0:T(8,128)S(1)} %bitcast.14), channel_id=1, source_target_pairs={{0,64},{64,0},{1,65},{65,1},{2,66},{66,2},{3,67},{67,3},{4,68},{68... | collective-permute-start | bytes 884744 | tf_op jit(solution)/shard_map/ppermute | solution.py:194
  96.6 1.2 %collective-permute-done.1.other_ref = f32[576,128]{1,0:T(8,128)S(1)} collective-permute-done((f32[576,128]{1,0:T(8,128)S(1)}, f32[576,128]{1,0:T(8,128)S(1)}, u32[]{:S(2)}, u32[]{:S(2)}) %collective-permute-start.1) | collective-permute-done | bytes 294944 | tf_op jit(solution)/shard_map/ppermute | solution.py:194
  97.7 0.0 copy-done
  97.7 6.9 %shard_map.29 = f32[64,1024]{1,0:T(8,128)S(1)} custom-call(s32[1]{0:T(128)} %bitcast.place_ref, f32[576,128]{1,0:T(8,128)S(1)} %bitcast.15, f32[576,128]{1,0:T(8,128)S(1)} %collective-permute-done.1.other_ref, f32[64,512]{1,0:T(8,128)S(1)} %bitcast.17, f32[512,1024]{1,0:T(8,128)S(1)} %bitcast.13), custom_call_target="tpu_custom_call" | custom-call | tf_op jit(solution)/shard_map/pallas_call | solution.py:196
  104.6 9.4 %all_to_all.28 = f32[8,8,1024]{2,1,0:T(8,128)S(1)} all-to-all(f32[8,8,1024]{2,1,0:T(8,128)S(1)} %bitcast.16), channel_id=1, replica_groups=mesh['y'=4,'core'=2,'z_mid'=4,'z_pair'=2,'x'=4,'z_hi'=2] {'y','core'}, dimensions={0} | all-to-all | bytes 524288 | tf_op jit(solution)/shard_map/all_to_all | solution.py:150
  114.0 0.7 copy.6
  (3 shorter events, 0.1 us)
Async XLA Ops:
  0.0 36.7 %all-to-all-start = ((f32[8,64,1024]{2,1,0:T(8,128)}), f32[8,64,1024]{2,1,0:T(8,128)S(1)}, u32[]{:S(2)}, u32[]{:S(2)}) async-start(f32[8,64,1024]{2,1,0:T(8,128)} %bitcast.18), calls=%async_computation | async-start | bytes 4194304 | tf_op jit(solution)/shard_map/all_to_all | solution.py:150
  36.7 61.0 %copy-start = (f32[512,64]{0,1:T(8,128)S(1)}, f32[512,64]{0,1:T(8,128)}, u32[]{:S(2)}) copy-start(f32[512,64]{0,1:T(8,128)} %param.3) | copy-start | bytes 393220
  38.3 4.0 %collective-permute-start = (f32[576,128]{1,0:T(8,128)S(1)}, f32[576,128]{1,0:T(8,128)S(1)}, u32[]{:S(2)}, u32[]{:S(2)}) collective-permute-start(f32[576,128]{1,0:T(8,128)S(1)} %get-tuple-element.8), channel_id=1, source_target_pairs={{0,64},{64,0},{1,65},{65,1},{2,66},{66,2},{3,67},{67,3},{4,68},{68... | collective-permute-start | bytes 884744 | tf_op jit(solution)/shard_map/ppermute | solution.py:188
  90.4 7.3 %collective-permute-start.1 = (f32[576,128]{1,0:T(8,128)S(1)}, f32[576,128]{1,0:T(8,128)S(1)}, u32[]{:S(2)}, u32[]{:S(2)}) collective-permute-start(f32[576,128]{1,0:T(8,128)S(1)} %bitcast.14), channel_id=1, source_target_pairs={{0,64},{64,0},{1,65},{65,1},{2,66},{66,2},{3,67},{67,3},{4,68},{68... | collective-permute-start | bytes 884744 | tf_op jit(solution)/shard_map/ppermute | solution.py:194

commit v10 on v9

--- a/solution.py
+++ b/solution.py
@@ -81,13 +81,14 @@
         row += LANES + HALF
 
 
-def inverse_factor(work, column_ref):
+def inverse_factor(work, column_ref, near_ref):
     n = work.shape[0]
     shape = (8, 2 * n)
     panels = n // 8
     tiles = [work[8 * k : 8 * k + 8] for k in range(panels)]
     sub = lax.broadcasted_iota(jnp.int32, shape, 0)
     done = []
+    ready = None
     for p in range(panels):
         at = n + 8 * p
         rest = range(p + 1, panels)
@@ -96,7 +97,8 @@
             return jnp.broadcast_to(tile[:, at + j : at + j + 1], shape)
 
         for j in range(8):
-            column_ref[p, j] = column(tiles[p], j)
+            column_ref[p, j] = column(tiles[p], j) if ready is None else ready[j]
+        ready = [column(tiles[p + 1], 8 + j) for j in range(8)] if rest else None
         rows = [jnp.broadcast_to(tiles[p][i : i + 1], shape) for i in range(8)]
         pivot = {
             (i, j): jnp.broadcast_to(column_ref[p, j, i : i + 1, :], shape)
@@ -114,6 +116,11 @@
                 for m in range(i + 1, j + 1):
                     pivot[j, m] = pivot[j, m] - factor[j, i] * pivot[m, i]
                 rows[j] = rows[j] - factor[j, i] * rows[i]
+            if rest:
+                near_ref[p, i] = below[p + 1][i]
+                for j in range(8):
+                    across = jnp.broadcast_to(near_ref[p, i, j : j + 1, :], shape)
+                    ready[j] = ready[j] - below[p + 1][i] * (across * inverse)
             for t in rest:
                 tiles[t] = tiles[t] - below[t][i] * scaled[i]
                 for j in range(i + 1, 8):
@@ -125,7 +132,7 @@
     return jnp.concatenate(done, axis=0)[:, :n]
 
 
-def core_kernel(place_ref, mine_ref, other_ref, start_ref, wide_ref, out_ref, gram_ref, full_ref, column_ref):
+def core_kernel(place_ref, mine_ref, other_ref, start_ref, wide_ref, out_ref, gram_ref, full_ref, column_ref, near_ref):
     size = mine_ref.shape[0]
     for part_ref, place in ((mine_ref, place_ref[0]), (other_ref, 1 - place_ref[0])):
         gram_ref[pl.ds(pl.multiple_of(place * size, 8), size), :] = part_ref[...]
@@ -142,7 +149,7 @@
     for step in range(ITERS):
         small = dot(image, jnp.concatenate([jnp.zeros_like(image), image], axis=0), across)
         follow = dot(image, full_ref[...] if step + 1 < ITERS else wide_ref[...], plain)
-        image = dot(inverse_factor(small + eye, column_ref), follow, plain)
+        image = dot(inverse_factor(small + eye, column_ref, near_ref), follow, plain)
     out_ref[...] = image
 
 
@@ -202,6 +209,7 @@
             pltpu.VMEM((depth, LANES), jnp.float32),
             pltpu.VMEM((order, order), jnp.float32),
             pltpu.VMEM((rank // 8, 8, 8, 2 * rank), jnp.float32),
+            pltpu.VMEM((rank // 8, 8, 8, 2 * rank), jnp.float32),
         ],
         compiler_params=params,
     )(place, mine, other, start.T, wide)

time: 115 us -> 114 us (level)
  no operation moved by 1% of the time
where the time goes in v10:
time: 114 us
  blocking collectives  57.3 us (50%)
  waiting for transfers between devices  28.7 us (25%)
  starting transfers between devices  19.3 us (17%)
  Pallas kernels  7.43 us (7%)
    all_to_all x4, blocking collectives, exchange(): return lax.all_to_all(x, axes, 0, 0, tiled=True)  57.3 us
    all_to_all x1, waiting for transfers between devices, exchange(): return lax.all_to_all(x, axes, 0, 0, tiled=True)  26.4 us
    all_to_all x1, starting transfers between devices, exchange(): return lax.all_to_all(x, axes, 0, 0, tiled=True)  10.4 us
    ppermute x1, starting transfers between devices, shards(): other = swap(mine)  6.13 us
    pallas_call x1, Pallas kernels, shards(): pl.pallas_call(core_kernel, in_specs=[scalar] + [VMEM] * 4, out_specs=VME...  5.92 us
    ppermute x1, starting transfers between devices, shards(): gram = (keep + swap(send)).reshape(depth // cores // SLAB, SLAB, LANES)  2.78 us
  transfers between devices with their start and end apart: 3, of which 3 were waited for; matrix products, arithmetic and copies ran while one was open for 0% of the time, Pallas kernels for 0%

profile of v10, /device:TPU:1, one launch (start us, length us, event | category | flops | bytes accessed | tf_op | source)
XLA Modules:
  0.0 113.7 jit_solution(4765230615296826491)
XLA Ops:
  0.0 10.4 %all-to-all-start = ((f32[8,64,1024]{2,1,0:T(8,128)}), f32[8,64,1024]{2,1,0:T(8,128)S(1)}, u32[]{:S(2)}, u32[]{:S(2)}) async-start(f32[8,64,1024]{2,1,0:T(8,128)} %bitcast.18), calls=%async_computation | async-start | bytes 4194304 | tf_op jit(solution)/shard_map/all_to_all | solution.py:157
  10.4 26.4 %all-to-all-done = f32[8,64,1024]{2,1,0:T(8,128)S(1)} async-done(((f32[8,64,1024]{2,1,0:T(8,128)}), f32[8,64,1024]{2,1,0:T(8,128)S(1)}, u32[]{:S(2)}, u32[]{:S(2)}) %all-to-all-start) | async-done | bytes 2097184 | tf_op jit(solution)/shard_map/all_to_all | solution.py:157
  36.7 0.0 copy-start
  36.7 1.5 %shard_map.28 = (f32[576,128]{1,0:T(8,128)S(1)}, f32[576,128]{1,0:T(8,128)S(1)}) custom-call(s32[1]{0:T(128)} %bitcast.place_ref, f32[512,1024]{1,0:T(8,128)S(1)} %bitcast.12), custom_call_target="tpu_custom_call" | custom-call | tf_op jit(solution)/shard_map/pallas_call | solution.py:185
  38.3 2.8 %collective-permute-start = (f32[576,128]{1,0:T(8,128)S(1)}, f32[576,128]{1,0:T(8,128)S(1)}, u32[]{:S(2)}, u32[]{:S(2)}) collective-permute-start(f32[576,128]{1,0:T(8,128)S(1)} %get-tuple-element.8), channel_id=1, source_target_pairs={{0,64},{64,0},{1,65},{65,1},{2,66},{66,2},{3,67},{67,3},{4,68},{68... | collective-permute-start | bytes 884744 | tf_op jit(solution)/shard_map/ppermute | solution.py:195
  41.0 1.2 %collective-permute-done = f32[576,128]{1,0:T(8,128)S(1)} collective-permute-done((f32[576,128]{1,0:T(8,128)S(1)}, f32[576,128]{1,0:T(8,128)S(1)}, u32[]{:S(2)}, u32[]{:S(2)}) %collective-permute-start) | collective-permute-done | bytes 294944 | tf_op jit(solution)/shard_map/ppermute | solution.py:195
  42.3 11.3 %all_to_all.25 = f32[288,2,128]{2,1,0:T(2,128)S(1)} all-to-all(f32[288,2,128]{2,1,0:T(2,128)S(1)} %bitcast.19), channel_id=1, replica_groups=mesh['y'=4,'core'=2,'z_mid'=4,'z_pair'=2,'x'=4,'z_hi'=2] {'y','z_pair','x'}, dimensions={0} | all-to-all | bytes 589824 | tf_op jit(solution)/shard_map/all_to_all | solution.py:157
  53.5 0.1 reduce_sum.18
  53.7 23.7 %all_to_all.26 = f32[72,2,128]{2,1,0:T(2,128)S(1)} all-to-all(f32[72,2,128]{2,1,0:T(2,128)S(1)} %bitcast.24), channel_id=1, replica_groups=mesh['y'=4,'core'=2,'z_mid'=4,'z_pair'=2,'x'=4,'z_hi'=2] {'z_mid','z_hi'}, dimensions={0} | all-to-all | bytes 147456 | tf_op jit(solution)/shard_map/all_to_all | solution.py:157
  77.4 0.1 broadcast_in_dim.7
  77.5 12.9 %all_to_all.27 = f32[288,2,128]{2,1,0:T(2,128)S(1)} all-to-all(f32[288,2,128]{2,1,0:T(2,128)S(1)} %bitcast.21), channel_id=1, replica_groups=mesh['y'=4,'core'=2,'z_mid'=4,'z_pair'=2,'x'=4,'z_hi'=2] {'y','z_pair','x'}, dimensions={0} | all-to-all | bytes 589824 | tf_op jit(solution)/shard_map/all_to_all | solution.py:157
  90.4 6.1 %collective-permute-start.1 = (f32[576,128]{1,0:T(8,128)S(1)}, f32[576,128]{1,0:T(8,128)S(1)}, u32[]{:S(2)}, u32[]{:S(2)}) collective-permute-start(f32[576,128]{1,0:T(8,128)S(1)} %bitcast.14), channel_id=1, source_target_pairs={{0,64},{64,0},{1,65},{65,1},{2,66},{66,2},{3,67},{67,3},{4,68},{68... | collective-permute-start | bytes 884744 | tf_op jit(solution)/shard_map/ppermute | solution.py:201
  96.6 1.2 %collective-permute-done.1.other_ref = f32[576,128]{1,0:T(8,128)S(1)} collective-permute-done((f32[576,128]{1,0:T(8,128)S(1)}, f32[576,128]{1,0:T(8,128)S(1)}, u32[]{:S(2)}, u32[]{:S(2)}) %collective-permute-start.1) | collective-permute-done | bytes 294944 | tf_op jit(solution)/shard_map/ppermute | solution.py:201
  97.7 0.0 copy-done
  97.7 5.9 %shard_map.29 = f32[64,1024]{1,0:T(8,128)S(1)} custom-call(s32[1]{0:T(128)} %bitcast.place_ref, f32[576,128]{1,0:T(8,128)S(1)} %bitcast.15, f32[576,128]{1,0:T(8,128)S(1)} %collective-permute-done.1.other_ref, f32[64,512]{1,0:T(8,128)S(1)} %bitcast.17, f32[512,1024]{1,0:T(8,128)S(1)} %bitcast.13), custom_call_target="tpu_custom_call" | custom-call | tf_op jit(solution)/shard_map/pallas_call | solution.py:203
  103.7 9.4 %all_to_all.28 = f32[8,8,1024]{2,1,0:T(8,128)S(1)} all-to-all(f32[8,8,1024]{2,1,0:T(8,128)S(1)} %bitcast.16), channel_id=1, replica_groups=mesh['y'=4,'core'=2,'z_mid'=4,'z_pair'=2,'x'=4,'z_hi'=2] {'y','core'}, dimensions={0} | all-to-all | bytes 524288 | tf_op jit(solution)/shard_map/all_to_all | solution.py:157
  113.0 0.7 copy.6
  (3 shorter events, 0.1 us)
Async XLA Ops:
  0.0 36.7 %all-to-all-start = ((f32[8,64,1024]{2,1,0:T(8,128)}), f32[8,64,1024]{2,1,0:T(8,128)S(1)}, u32[]{:S(2)}, u32[]{:S(2)}) async-start(f32[8,64,1024]{2,1,0:T(8,128)} %bitcast.18), calls=%async_computation | async-start | bytes 4194304 | tf_op jit(solution)/shard_map/all_to_all | solution.py:157
  36.7 61.0 %copy-start = (f32[512,64]{0,1:T(8,128)S(1)}, f32[512,64]{0,1:T(8,128)}, u32[]{:S(2)}) copy-start(f32[512,64]{0,1:T(8,128)} %param.3) | copy-start | bytes 393220
  38.3 4.0 %collective-permute-start = (f32[576,128]{1,0:T(8,128)S(1)}, f32[576,128]{1,0:T(8,128)S(1)}, u32[]{:S(2)}, u32[]{:S(2)}) collective-permute-start(f32[576,128]{1,0:T(8,128)S(1)} %get-tuple-element.8), channel_id=1, source_target_pairs={{0,64},{64,0},{1,65},{65,1},{2,66},{66,2},{3,67},{67,3},{4,68},{68... | collective-permute-start | bytes 884744 | tf_op jit(solution)/shard_map/ppermute | solution.py:195
  90.4 7.3 %collective-permute-start.1 = (f32[576,128]{1,0:T(8,128)S(1)}, f32[576,128]{1,0:T(8,128)S(1)}, u32[]{:S(2)}, u32[]{:S(2)}) collective-permute-start(f32[576,128]{1,0:T(8,128)S(1)} %bitcast.14), channel_id=1, source_target_pairs={{0,64},{64,0},{1,65},{65,1},{2,66},{66,2},{3,67},{67,3},{4,68},{68... | collective-permute-start | bytes 884744 | tf_op jit(solution)/shard_map/ppermute | solution.py:201

commit v11 on v10

--- a/solution.py
+++ b/solution.py
@@ -38,7 +38,9 @@
     for i in range(2):
         for j in range(i, 2):
             a, b = slice(i * half, (i + 1) * half), slice(j * half, (j + 1) * half)
-            parts[i, j] = dot(high[a], high[b]) + (dot(high[a], low[b]) + dot(low[a], high[b]))
+            mixed = dot(high[a], low[b])
+            mirror = mixed.T if i == j else dot(low[a], high[b])
+            parts[i, j] = dot(high[a], high[b]) + (mixed + mirror)
     per = half // LANES
     row = 0
 

time: 114 us -> 114 us (level)
  no operation moved by 1% of the time
where the time goes in v11:
time: 114 us; the launch traced here: 113 us
  blocking collectives  57.3 us (50%)
  waiting for transfers between devices  28.7 us (25%)
  starting transfers between devices  19.3 us (17%)
  Pallas kernels  7.16 us (6%)
    all_to_all x4, blocking collectives, exchange(): return lax.all_to_all(x, axes, 0, 0, tiled=True)  57.3 us
    all_to_all x1, waiting for transfers between devices, exchange(): return lax.all_to_all(x, axes, 0, 0, tiled=True)  26.4 us
    all_to_all x1, starting transfers between devices, exchange(): return lax.all_to_all(x, axes, 0, 0, tiled=True)  10.4 us
    ppermute x1, starting transfers between devices, shards(): other = swap(mine)  6.13 us
    pallas_call x1, Pallas kernels, shards(): pl.pallas_call(core_kernel, in_specs=[scalar] + [VMEM] * 4, out_specs=VME...  5.93 us
    ppermute x1, starting transfers between devices, shards(): gram = (keep + swap(send)).reshape(depth // cores // SLAB, SLAB, LANES)  2.79 us
  transfers between devices with their start and end apart: 3, of which 3 were waited for; matrix products, arithmetic and copies ran while one was open for 0% of the time, Pallas kernels for 0%

profile of v11, /device:TPU:1, one launch (start us, length us, event | category | flops | bytes accessed | tf_op | source)
XLA Modules:
  0.0 113.5 jit_solution(8062764212830238702)
XLA Ops:
  0.0 10.4 %all-to-all-start = ((f32[8,64,1024]{2,1,0:T(8,128)}), f32[8,64,1024]{2,1,0:T(8,128)S(1)}, u32[]{:S(2)}, u32[]{:S(2)}) async-start(f32[8,64,1024]{2,1,0:T(8,128)} %bitcast.18), calls=%async_computation | async-start | bytes 4194304 | tf_op jit(solution)/shard_map/all_to_all | solution.py:159
  10.4 26.4 %all-to-all-done = f32[8,64,1024]{2,1,0:T(8,128)S(1)} async-done(((f32[8,64,1024]{2,1,0:T(8,128)}), f32[8,64,1024]{2,1,0:T(8,128)S(1)}, u32[]{:S(2)}, u32[]{:S(2)}) %all-to-all-start) | async-done | bytes 2097184 | tf_op jit(solution)/shard_map/all_to_all | solution.py:159
  36.7 0.0 copy-start
  36.7 1.2 %shard_map.28 = (f32[576,128]{1,0:T(8,128)S(1)}, f32[576,128]{1,0:T(8,128)S(1)}) custom-call(s32[1]{0:T(128)} %bitcast.place_ref, f32[512,1024]{1,0:T(8,128)S(1)} %bitcast.12), custom_call_target="tpu_custom_call" | custom-call | tf_op jit(solution)/shard_map/pallas_call | solution.py:187
  38.0 2.8 %collective-permute-start = (f32[576,128]{1,0:T(8,128)S(1)}, f32[576,128]{1,0:T(8,128)S(1)}, u32[]{:S(2)}, u32[]{:S(2)}) collective-permute-start(f32[576,128]{1,0:T(8,128)S(1)} %get-tuple-element.8), channel_id=1, source_target_pairs={{0,64},{64,0},{1,65},{65,1},{2,66},{66,2},{3,67},{67,3},{4,68},{68... | collective-permute-start | bytes 884744 | tf_op jit(solution)/shard_map/ppermute | solution.py:197
  40.8 1.2 %collective-permute-done = f32[576,128]{1,0:T(8,128)S(1)} collective-permute-done((f32[576,128]{1,0:T(8,128)S(1)}, f32[576,128]{1,0:T(8,128)S(1)}, u32[]{:S(2)}, u32[]{:S(2)}) %collective-permute-start) | collective-permute-done | bytes 294944 | tf_op jit(solution)/shard_map/ppermute | solution.py:197
  42.0 11.3 %all_to_all.25 = f32[288,2,128]{2,1,0:T(2,128)S(1)} all-to-all(f32[288,2,128]{2,1,0:T(2,128)S(1)} %bitcast.19), channel_id=1, replica_groups=mesh['y'=4,'core'=2,'z_mid'=4,'z_pair'=2,'x'=4,'z_hi'=2] {'y','z_pair','x'}, dimensions={0} | all-to-all | bytes 589824 | tf_op jit(solution)/shard_map/all_to_all | solution.py:159
  53.3 0.1 reduce_sum.18
  53.4 23.7 %all_to_all.26 = f32[72,2,128]{2,1,0:T(2,128)S(1)} all-to-all(f32[72,2,128]{2,1,0:T(2,128)S(1)} %bitcast.24), channel_id=1, replica_groups=mesh['y'=4,'core'=2,'z_mid'=4,'z_pair'=2,'x'=4,'z_hi'=2] {'z_mid','z_hi'}, dimensions={0} | all-to-all | bytes 147456 | tf_op jit(solution)/shard_map/all_to_all | solution.py:159
  77.2 0.1 broadcast_in_dim.7
  77.2 12.9 %all_to_all.27 = f32[288,2,128]{2,1,0:T(2,128)S(1)} all-to-all(f32[288,2,128]{2,1,0:T(2,128)S(1)} %bitcast.21), channel_id=1, replica_groups=mesh['y'=4,'core'=2,'z_mid'=4,'z_pair'=2,'x'=4,'z_hi'=2] {'y','z_pair','x'}, dimensions={0} | all-to-all | bytes 589824 | tf_op jit(solution)/shard_map/all_to_all | solution.py:159
  90.1 6.1 %collective-permute-start.1 = (f32[576,128]{1,0:T(8,128)S(1)}, f32[576,128]{1,0:T(8,128)S(1)}, u32[]{:S(2)}, u32[]{:S(2)}) collective-permute-start(f32[576,128]{1,0:T(8,128)S(1)} %bitcast.14), channel_id=1, source_target_pairs={{0,64},{64,0},{1,65},{65,1},{2,66},{66,2},{3,67},{67,3},{4,68},{68... | collective-permute-start | bytes 884744 | tf_op jit(solution)/shard_map/ppermute | solution.py:203
  96.3 1.2 %collective-permute-done.1.other_ref = f32[576,128]{1,0:T(8,128)S(1)} collective-permute-done((f32[576,128]{1,0:T(8,128)S(1)}, f32[576,128]{1,0:T(8,128)S(1)}, u32[]{:S(2)}, u32[]{:S(2)}) %collective-permute-start.1) | collective-permute-done | bytes 294944 | tf_op jit(solution)/shard_map/ppermute | solution.py:203
  97.5 0.0 copy-done
  97.5 5.9 %shard_map.29 = f32[64,1024]{1,0:T(8,128)S(1)} custom-call(s32[1]{0:T(128)} %bitcast.place_ref, f32[576,128]{1,0:T(8,128)S(1)} %bitcast.15, f32[576,128]{1,0:T(8,128)S(1)} %collective-permute-done.1.other_ref, f32[64,512]{1,0:T(8,128)S(1)} %bitcast.17, f32[512,1024]{1,0:T(8,128)S(1)} %bitcast.13), custom_call_target="tpu_custom_call" | custom-call | tf_op jit(solution)/shard_map/pallas_call | solution.py:205
  103.4 9.4 %all_to_all.28 = f32[8,8,1024]{2,1,0:T(8,128)S(1)} all-to-all(f32[8,8,1024]{2,1,0:T(8,128)S(1)} %bitcast.16), channel_id=1, replica_groups=mesh['y'=4,'core'=2,'z_mid'=4,'z_pair'=2,'x'=4,'z_hi'=2] {'y','core'}, dimensions={0} | all-to-all | bytes 524288 | tf_op jit(solution)/shard_map/all_to_all | solution.py:159
  112.8 0.7 copy.6
  (3 shorter events, 0.1 us)
Async XLA Ops:
  0.0 36.7 %all-to-all-start = ((f32[8,64,1024]{2,1,0:T(8,128)}), f32[8,64,1024]{2,1,0:T(8,128)S(1)}, u32[]{:S(2)}, u32[]{:S(2)}) async-start(f32[8,64,1024]{2,1,0:T(8,128)} %bitcast.18), calls=%async_computation | async-start | bytes 4194304 | tf_op jit(solution)/shard_map/all_to_all | solution.py:159
  36.7 60.7 %copy-start = (f32[512,64]{0,1:T(8,128)S(1)}, f32[512,64]{0,1:T(8,128)}, u32[]{:S(2)}) copy-start(f32[512,64]{0,1:T(8,128)} %param.3) | copy-start | bytes 393220
  38.0 4.0 %collective-permute-start = (f32[576,128]{1,0:T(8,128)S(1)}, f32[576,128]{1,0:T(8,128)S(1)}, u32[]{:S(2)}, u32[]{:S(2)}) collective-permute-start(f32[576,128]{1,0:T(8,128)S(1)} %get-tuple-element.8), channel_id=1, source_target_pairs={{0,64},{64,0},{1,65},{65,1},{2,66},{66,2},{3,67},{67,3},{4,68},{68... | collective-permute-start | bytes 884744 | tf_op jit(solution)/shard_map/ppermute | solution.py:197
  90.1 7.3 %collective-permute-start.1 = (f32[576,128]{1,0:T(8,128)S(1)}, f32[576,128]{1,0:T(8,128)S(1)}, u32[]{:S(2)}, u32[]{:S(2)}) collective-permute-start(f32[576,128]{1,0:T(8,128)S(1)} %bitcast.14), channel_id=1, source_target_pairs={{0,64},{64,0},{1,65},{65,1},{2,66},{66,2},{3,67},{67,3},{4,68},{68... | collective-permute-start | bytes 884744 | tf_op jit(solution)/shard_map/ppermute | solution.py:203

commit v12 on v11

--- a/solution.py
+++ b/solution.py
@@ -234,7 +234,7 @@
             count,
             ("y", "core"),
             "core",
-            ("y", "z_pair", "x"),
+            ("x", "z_pair", "y"),
             ("z_mid", "z_hi"),
         )
         return jax.shard_map(

time: 114 us -> 114 us (level)
  no operation moved by 1% of the time
where the time goes in v12:
time: 114 us; the launch traced here: 113 us
  blocking collectives  56.9 us (50%)
  waiting for transfers between devices  28.7 us (25%)
  starting transfers between devices  19.5 us (17%)
  Pallas kernels  7.15 us (6%)
    all_to_all x4, blocking collectives, exchange(): return lax.all_to_all(x, axes, 0, 0, tiled=True)  56.9 us
    all_to_all x1, waiting for transfers between devices, exchange(): return lax.all_to_all(x, axes, 0, 0, tiled=True)  26.4 us
    all_to_all x1, starting transfers between devices, exchange(): return lax.all_to_all(x, axes, 0, 0, tiled=True)  10.4 us
    ppermute x1, starting transfers between devices, shards(): other = swap(mine)  6.32 us
    pallas_call x1, Pallas kernels, shards(): pl.pallas_call(core_kernel, in_specs=[scalar] + [VMEM] * 4, out_specs=VME...  5.92 us
    ppermute x1, starting transfers between devices, shards(): gram = (keep + swap(send)).reshape(depth // cores // SLAB, SLAB, LANES)  2.79 us
  transfers between devices with their start and end apart: 3, of which 3 were waited for; matrix products, arithmetic and copies ran while one was open for 0% of the time, Pallas kernels for 0%

profile of v12, /device:TPU:1, one launch (start us, length us, event | category | flops | bytes accessed | tf_op | source)
XLA Modules:
  0.0 113.3 jit_solution(18052072829985837356)
XLA Ops:
  0.0 10.4 %all-to-all-start = ((f32[8,64,1024]{2,1,0:T(8,128)}), f32[8,64,1024]{2,1,0:T(8,128)S(1)}, u32[]{:S(2)}, u32[]{:S(2)}) async-start(f32[8,64,1024]{2,1,0:T(8,128)} %bitcast.18), calls=%async_computation | async-start | bytes 4194304 | tf_op jit(solution)/shard_map/all_to_all | solution.py:159
  10.4 26.4 %all-to-all-done = f32[8,64,1024]{2,1,0:T(8,128)S(1)} async-done(((f32[8,64,1024]{2,1,0:T(8,128)}), f32[8,64,1024]{2,1,0:T(8,128)S(1)}, u32[]{:S(2)}, u32[]{:S(2)}) %all-to-all-start) | async-done | bytes 2097184 | tf_op jit(solution)/shard_map/all_to_all | solution.py:159
  36.7 0.0 copy-start
  36.7 1.2 %shard_map.28 = (f32[576,128]{1,0:T(8,128)S(1)}, f32[576,128]{1,0:T(8,128)S(1)}) custom-call(s32[1]{0:T(128)} %bitcast.place_ref, f32[512,1024]{1,0:T(8,128)S(1)} %bitcast.12), custom_call_target="tpu_custom_call" | custom-call | tf_op jit(solution)/shard_map/pallas_call | solution.py:187
  38.0 2.8 %collective-permute-start = (f32[576,128]{1,0:T(8,128)S(1)}, f32[576,128]{1,0:T(8,128)S(1)}, u32[]{:S(2)}, u32[]{:S(2)}) collective-permute-start(f32[576,128]{1,0:T(8,128)S(1)} %get-tuple-element.8), channel_id=1, source_target_pairs={{0,64},{64,0},{1,65},{65,1},{2,66},{66,2},{3,67},{67,3},{4,68},{68... | collective-permute-start | bytes 884744 | tf_op jit(solution)/shard_map/ppermute | solution.py:197
  40.8 1.2 %collective-permute-done = f32[576,128]{1,0:T(8,128)S(1)} collective-permute-done((f32[576,128]{1,0:T(8,128)S(1)}, f32[576,128]{1,0:T(8,128)S(1)}, u32[]{:S(2)}, u32[]{:S(2)}) %collective-permute-start) | collective-permute-done | bytes 294944 | tf_op jit(solution)/shard_map/ppermute | solution.py:197
  42.0 11.4 %all_to_all.25 = f32[288,2,128]{2,1,0:T(2,128)S(1)} all-to-all(f32[288,2,128]{2,1,0:T(2,128)S(1)} %bitcast.19), channel_id=1, replica_groups=mesh['y'=4,'core'=2,'z_mid'=4,'z_pair'=2,'x'=4,'z_hi'=2] {'x','z_pair','y'}, dimensions={0} | all-to-all | bytes 589824 | tf_op jit(solution)/shard_map/all_to_all | solution.py:159
  53.4 0.1 reduce_sum.18
  53.5 23.7 %all_to_all.26 = f32[72,2,128]{2,1,0:T(2,128)S(1)} all-to-all(f32[72,2,128]{2,1,0:T(2,128)S(1)} %bitcast.24), channel_id=1, replica_groups=mesh['y'=4,'core'=2,'z_mid'=4,'z_pair'=2,'x'=4,'z_hi'=2] {'z_mid','z_hi'}, dimensions={0} | all-to-all | bytes 147456 | tf_op jit(solution)/shard_map/all_to_all | solution.py:159
  77.2 0.1 broadcast_in_dim.7
  77.3 12.3 %all_to_all.27 = f32[288,2,128]{2,1,0:T(2,128)S(1)} all-to-all(f32[288,2,128]{2,1,0:T(2,128)S(1)} %bitcast.21), channel_id=1, replica_groups=mesh['y'=4,'core'=2,'z_mid'=4,'z_pair'=2,'x'=4,'z_hi'=2] {'x','z_pair','y'}, dimensions={0} | all-to-all | bytes 589824 | tf_op jit(solution)/shard_map/all_to_all | solution.py:159
  89.6 6.3 %collective-permute-start.1 = (f32[576,128]{1,0:T(8,128)S(1)}, f32[576,128]{1,0:T(8,128)S(1)}, u32[]{:S(2)}, u32[]{:S(2)}) collective-permute-start(f32[576,128]{1,0:T(8,128)S(1)} %bitcast.14), channel_id=1, source_target_pairs={{0,64},{64,0},{1,65},{65,1},{2,66},{66,2},{3,67},{67,3},{4,68},{68... | collective-permute-start | bytes 884744 | tf_op jit(solution)/shard_map/ppermute | solution.py:203
  95.9 1.2 %collective-permute-done.1.other_ref = f32[576,128]{1,0:T(8,128)S(1)} collective-permute-done((f32[576,128]{1,0:T(8,128)S(1)}, f32[576,128]{1,0:T(8,128)S(1)}, u32[]{:S(2)}, u32[]{:S(2)}) %collective-permute-start.1) | collective-permute-done | bytes 294944 | tf_op jit(solution)/shard_map/ppermute | solution.py:203
  97.1 0.0 copy-done
  97.1 5.9 %shard_map.29 = f32[64,1024]{1,0:T(8,128)S(1)} custom-call(s32[1]{0:T(128)} %bitcast.place_ref, f32[576,128]{1,0:T(8,128)S(1)} %bitcast.15, f32[576,128]{1,0:T(8,128)S(1)} %collective-permute-done.1.other_ref, f32[64,512]{1,0:T(8,128)S(1)} %bitcast.17, f32[512,1024]{1,0:T(8,128)S(1)} %bitcast.13), custom_call_target="tpu_custom_call" | custom-call | tf_op jit(solution)/shard_map/pallas_call | solution.py:205
  103.1 9.5 %all_to_all.28 = f32[8,8,1024]{2,1,0:T(8,128)S(1)} all-to-all(f32[8,8,1024]{2,1,0:T(8,128)S(1)} %bitcast.16), channel_id=1, replica_groups=mesh['y'=4,'core'=2,'z_mid'=4,'z_pair'=2,'x'=4,'z_hi'=2] {'y','core'}, dimensions={0} | all-to-all | bytes 524288 | tf_op jit(solution)/shard_map/all_to_all | solution.py:159
  112.6 0.7 copy.6
  (3 shorter events, 0.1 us)
Async XLA Ops:
  0.0 36.7 %all-to-all-start = ((f32[8,64,1024]{2,1,0:T(8,128)}), f32[8,64,1024]{2,1,0:T(8,128)S(1)}, u32[]{:S(2)}, u32[]{:S(2)}) async-start(f32[8,64,1024]{2,1,0:T(8,128)} %bitcast.18), calls=%async_computation | async-start | bytes 4194304 | tf_op jit(solution)/shard_map/all_to_all | solution.py:159
  36.7 60.4 %copy-start = (f32[512,64]{0,1:T(8,128)S(1)}, f32[512,64]{0,1:T(8,128)}, u32[]{:S(2)}) copy-start(f32[512,64]{0,1:T(8,128)} %param.3) | copy-start | bytes 393220
  38.0 4.0 %collective-permute-start = (f32[576,128]{1,0:T(8,128)S(1)}, f32[576,128]{1,0:T(8,128)S(1)}, u32[]{:S(2)}, u32[]{:S(2)}) collective-permute-start(f32[576,128]{1,0:T(8,128)S(1)} %get-tuple-element.8), channel_id=1, source_target_pairs={{0,64},{64,0},{1,65},{65,1},{2,66},{66,2},{3,67},{67,3},{4,68},{68... | collective-permute-start | bytes 884744 | tf_op jit(solution)/shard_map/ppermute | solution.py:197
  89.6 7.5 %collective-permute-start.1 = (f32[576,128]{1,0:T(8,128)S(1)}, f32[576,128]{1,0:T(8,128)S(1)}, u32[]{:S(2)}, u32[]{:S(2)}) collective-permute-start(f32[576,128]{1,0:T(8,128)S(1)} %bitcast.14), channel_id=1, source_target_pairs={{0,64},{64,0},{1,65},{65,1},{2,66},{66,2},{3,67},{67,3},{4,68},{68... | collective-permute-start | bytes 884744 | tf_op jit(solution)/shard_map/ppermute | solution.py:203
